TPU v7x, 512 devices: a whole 4x8x8 slice. The times are simulated.
512 devices in a mesh: seq: 8 (over z_lo, core), vocab: 64 (over y, x, z_hi).
Axes of the slice: x: 4, y: 8, z: 8 (z_hi: 2, z_lo: 4; z = z_hi * 4 + z_lo), core: 2. Of those that a mesh axis runs over, the one named last changes fastest.
Arguments:
- posteriors: bfloat16 [32768, 16384], P(('seq', 'vocab')), may hold values from 0.2 to 2300, as said below
- token_block: int32 [32768, 1], P(('seq', 'vocab')), may hold values from 0 to 63; in each aligned block of 64 rows (0 to 63, 64 to 127, ...) at most 2 rows name the same one
- token_offset: int32 [32768], P(('seq', 'vocab')), may hold values from 0 to 255
- lengths: int32 [8], replicated, may hold values from 2048 to 4096, as said below
- smoothing: float32 [16384], P('seq'), may hold values from 4 to 40
Outputs:
- emission: float32 [16384, 16384], P('seq', 'vocab')
Inputs may be any that keep to these rules, and one draw needn't show every extreme that they name: `posteriors`: all entries are positive. `lengths`: some group is live over all its positions.
All inputs are finite; a program needn't handle non-finite values.
Results may differ from a plain program's by a relative error of at most 0.0003.
Values may be sent and summed in bfloat16 or wider, within the bound.
No kernel may reach another device: no remote copies, remote signals or barrier semaphores. Data moves between devices by JAX's collectives and lax.ppermute only.
A program may use at most 64 MiB of HBM per device.

v0:
```python
import jax
import jax.numpy as jnp
from jax import lax
from jax.sharding import PartitionSpec as P

VOCAB = 16384


def shards(posteriors, token_block, token_offset, lengths, smoothing):
    tok_rows, states = posteriors.shape
    vocab_devs = lax.axis_size("vocab")
    seq_devs = lax.axis_size("seq")
    capacity = 2 * tok_rows // vocab_devs
    width_local = VOCAB // vocab_devs
    state_rows = states // seq_devs
    position_ratio = tok_rows * vocab_devs * seq_devs / VOCAB
    position = lax.axis_index("vocab") * tok_rows + jnp.arange(tok_rows, dtype=jnp.int32)
    length_limit = lengths[lax.axis_index("seq")]
    keep_row = (position < length_limit).astype(jnp.bfloat16)
    masked = posteriors * keep_row[:, None]
    owner_block = token_block[:, 0]
    block_hits = (owner_block[:, None] == jnp.arange(vocab_devs, dtype=jnp.int32)[None, :]).astype(
        jnp.int32
    )
    slot_rank = jnp.sum(jnp.cumsum(block_hits, axis=0) * block_hits, axis=1) - 1
    slot_index = owner_block * capacity + slot_rank
    buckets = jnp.zeros((vocab_devs * capacity, states), jnp.bfloat16).at[slot_index].set(masked)
    buckets = buckets.reshape(vocab_devs, capacity, states)
    halves = jnp.stack(
        [(token_offset // 16).astype(jnp.float32), (token_offset % 16).astype(jnp.float32)], axis=-1
    )
    slot_halves = jnp.zeros((vocab_devs * capacity, 2), jnp.float32).at[slot_index].set(halves)
    offset_tags = jnp.tile(slot_halves.reshape(vocab_devs, capacity, 1, 2), (1, 1, seq_devs, 1))
    offset_tags = offset_tags.reshape(vocab_devs, capacity, 2 * seq_devs).astype(jnp.bfloat16)
    first_rows, first_tags = (
        lax.all_to_all(buckets, "vocab", split_axis=0, concat_axis=0, tiled=True),
        lax.all_to_all(offset_tags, "vocab", split_axis=0, concat_axis=0, tiled=True),
    )
    received, tag_values = (
        lax.all_to_all(first_rows, "seq", split_axis=2, concat_axis=1, tiled=True),
        lax.all_to_all(first_tags, "seq", split_axis=2, concat_axis=1, tiled=True),
    )
    received = received.reshape(-1, state_rows)
    tag_values = tag_values.reshape(-1, 2).astype(jnp.float32)
    local_offset = tag_values[:, 0] * 16.0 + tag_values[:, 1]
    one_hot = (local_offset[:, None] == jnp.arange(width_local, dtype=jnp.float32)[None, :]).astype(
        jnp.bfloat16
    )
    counts = lax.dot_general(
        received, one_hot, (((0,), (0,)), ((), ())), preferred_element_type=jnp.float32
    )
    totals = lax.psum(jnp.sum(counts, axis=1), "vocab")
    pseudo = smoothing * position_ratio
    emission = VOCAB * (counts + pseudo[:, None]) / (totals[:, None] + VOCAB * pseudo[:, None])
    return emission


def solution(mesh):
    placed = (
        P(("seq", "vocab"), None),
        P(("seq", "vocab"), None),
        P(("seq", "vocab")),
        P(),
        P("seq"),
    )
    return jax.shard_map(
        shards, mesh=mesh, in_specs=placed, out_specs=P("seq", "vocab"), check_vma=False
    )
```

profile of v0, /device:TPU:64, one launch (start us, length us, event | category | flops | bytes accessed | tf_op | source)
XLA Modules:
  0.0 554.5 jit_solution(1916767340823525059)
XLA Ops:
  0.0 0.7 fusion.8
  0.7 0.1 reduce_window_sum.11
  0.8 0.8 select_reduce_fusion
  1.7 0.7 fusion.11
  2.3 0.7 convert_bitcast_fusion.1
  3.0 0.1 copy.22
  3.1 0.8 scatter_custom_fusion.1
  3.9 0.1 copy.23
  4.0 0.7 copy.24
  4.7 18.1 %all-to-all-start.2 = ((bf16[64,2,16]{2,1,0:T(2,128)(2,1)}), bf16[64,2,16]{2,1,0:T(2,128)(2,1)S(1)}, u32[]{:S(2)}, u32[]{:S(2)}) async-start(bf16[64,2,16]{2,1,0:T(2,128)(2,1)} %copy.24), calls=%async_computation.2 | async-start | bytes 65536 | tf_op jit(solution)/shard_map/all_to_all | solution.py:37
  22.9 1.3 dynamic_slice.3
  24.2 0.7 compare_convert_fusion
  24.9 7.1 %scatter_custom_fusion = bf16[128,16384]{1,0:T(8,128)(2,1)} fusion(s32[64]{0:T(128)S(1)} %fusion.11, bf16[64,16384]{1,0:T(8,128)(2,1)} %param.5, bf16[]{:T(256)} %constant.48.clone.1, bf16[64]{0:T(256)(128)(2,1)S(1)} %compare_convert_fusion), kind=kCustom, calls=%fused_computation.3 | custom fusion | flops 1048576 | bytes 6291970 | tf_op jit(solution)/shard_map/scatter | solution.py:27
  31.9 7.6 %reshape.38 = bf16[64,2,16384]{2,1,0:T(2,128)(2,1)} reshape(bf16[128,16384]{1,0:T(8,128)(2,1)} %scatter_custom_fusion) | data formatting | bytes 8388608 | tf_op jit(solution)/shard_map/reshape | solution.py:28
  39.5 0.0 all-to-all-done.2
  39.5 15.4 %all-to-all-start = ((bf16[64,2,16384]{2,1,0:T(2,128)(2,1)}), bf16[64,2,16384]{2,1,0:T(2,128)(2,1)}, u32[]{:S(2)}, u32[]{:S(2)}) async-start(bf16[64,2,16384]{2,1,0:T(2,128)(2,1)} %reshape.38), calls=%async_computation | async-start | bytes 8388608 | tf_op jit(solution)/shard_map/all_to_all | solution.py:36
  54.9 0.1 copy.25
  55.0 0.7 reshape.64
  55.7 97.0 %all-to-all-done = bf16[64,2,16384]{2,1,0:T(2,128)(2,1)} async-done(((bf16[64,2,16384]{2,1,0:T(2,128)(2,1)}), bf16[64,2,16384]{2,1,0:T(2,128)(2,1)}, u32[]{:S(2)}, u32[]{:S(2)}) %all-to-all-start) | async-done | bytes 4194336 | tf_op jit(solution)/shard_map/all_to_all | solution.py:36
  152.7 6.3 %all-to-all-start.3 = ((bf16[8,2,128]{2,1,0:T(2,128)(2,1)}), bf16[8,2,128]{2,1,0:T(2,128)(2,1)S(1)}, u32[]{:S(2)}, u32[]{:S(2)}) async-start(bf16[8,2,128]{2,1,0:T(2,128)(2,1)} %reshape.64), calls=%async_computation.3 | async-start | bytes 8192 | tf_op jit(solution)/shard_map/all_to_all | solution.py:41
  159.0 21.6 %copy.20 = bf16[64,2,16384]{0,1,2:T(2,128)(2,1)} copy(bf16[64,2,16384]{2,1,0:T(2,128)(2,1)} %all-to-all-done) | data formatting | bytes 8388608 | tf_op jit(solution)/shard_map/all_to_all | solution.py:36
  180.6 10.5 %reshape.62 = bf16[8,2,131072]{2,1,0:T(2,128)(2,1)} reshape(bf16[16384,2,64]{2,1,0:T(2,128)(2,1)} %bitcast.30) | data formatting | bytes 8388608
  191.1 0.0 all-to-all-done.3
  191.1 5.1 all-to-all-start.1
  196.2 0.1 reshape.65
  196.3 0.3 copy.27
  196.6 0.3 reshape.40
  196.9 89.8 %all-to-all-done.1 = bf16[8,2,131072]{2,1,0:T(2,128)(2,1)} async-done(((bf16[8,2,131072]{2,1,0:T(2,128)(2,1)}), bf16[8,2,131072]{2,1,0:T(2,128)(2,1)}, u32[]{:S(2)}, u32[]{:S(2)}) %all-to-all-start.1) | async-done | bytes 4194336 | tf_op jit(solution)/shard_map/all_to_all | solution.py:40
  286.7 10.3 %reshape.63 = bf16[16384,2,64]{2,1,0:T(2,128)(2,1)} reshape(bf16[8,2,131072]{2,1,0:T(2,128)(2,1)} %all-to-all-done.1) | data formatting | bytes 8388608
  297.0 21.1 %copy.21 = bf16[64,2,8,2048]{3,1,2,0:T(2,128)(2,1)} copy(bf16[64,2,8,2048]{0,1,3,2:T(2,128)(2,1)} %bitcast.31) | data formatting | bytes 8388608 | tf_op jit(solution)/shard_map/all_to_all | solution.py:40
  318.2 7.2 %reshape.39 = bf16[1024,2048]{1,0:T(8,128)(2,1)} reshape(bf16[64,8,2,2048]{3,2,1,0:T(2,128)(2,1)} %bitcast.32) | data formatting | bytes 8388608 | tf_op jit(solution)/shard_map/reshape | solution.py:43
  325.4 0.0 copy-start
  325.4 4.9 fusion.12
  330.3 220.5 %psum.7 = f32[2048]{0:T(1024)S(1)} all-reduce(f32[2048]{0:T(1024)S(1)} %get-tuple-element.9), channel_id=1, replica_groups=mesh['seq'=8,'vocab'=64] {'vocab'}, use_global_device_ids=true, to_apply=%region_5.6 | all-reduce | flops 2048 | bytes 16384 | tf_op jit(solution)/shard_map/psum | solution.py:52
  550.8 0.0 copy-done
  550.8 1.9 multiply_divide_fusion
  552.7 1.8 copy.28
  (7 shorter events, 0.1 us)
Async XLA Ops:
  4.7 34.8 %all-to-all-start.2 = ((bf16[64,2,16]{2,1,0:T(2,128)(2,1)}), bf16[64,2,16]{2,1,0:T(2,128)(2,1)S(1)}, u32[]{:S(2)}, u32[]{:S(2)}) async-start(bf16[64,2,16]{2,1,0:T(2,128)(2,1)} %copy.24), calls=%async_computation.2 | async-start | bytes 65536 | tf_op jit(solution)/shard_map/all_to_all | solution.py:37
  39.5 113.1 %all-to-all-start = ((bf16[64,2,16384]{2,1,0:T(2,128)(2,1)}), bf16[64,2,16384]{2,1,0:T(2,128)(2,1)}, u32[]{:S(2)}, u32[]{:S(2)}) async-start(bf16[64,2,16384]{2,1,0:T(2,128)(2,1)} %reshape.38), calls=%async_computation | async-start | bytes 8388608 | tf_op jit(solution)/shard_map/all_to_all | solution.py:36
  152.7 38.4 %all-to-all-start.3 = ((bf16[8,2,128]{2,1,0:T(2,128)(2,1)}), bf16[8,2,128]{2,1,0:T(2,128)(2,1)S(1)}, u32[]{:S(2)}, u32[]{:S(2)}) async-start(bf16[8,2,128]{2,1,0:T(2,128)(2,1)} %reshape.64), calls=%async_computation.3 | async-start | bytes 8192 | tf_op jit(solution)/shard_map/all_to_all | solution.py:41
  191.1 95.6 %all-to-all-start.1 = ((bf16[8,2,131072]{2,1,0:T(2,128)(2,1)}), bf16[8,2,131072]{2,1,0:T(2,128)(2,1)}, u32[]{:S(2)}, u32[]{:S(2)}) async-start(bf16[8,2,131072]{2,1,0:T(2,128)(2,1)} %reshape.62), calls=%async_computation.1 | async-start | bytes 8388608 | tf_op jit(solution)/shard_map/all_to_all | solution.py:40
  325.4 225.4 %copy-start = (f32[2048]{0:T(1024)S(1)}, f32[2048]{0:T(1024)}, u32[]{:S(2)}) copy-start(f32[2048]{0:T(1024)} %param.9) | copy-start | bytes 24580
where the time goes:
time: 557 us; the launch traced here: 555 us
  blocking collectives  220 us (39%)
  waiting for transfers between devices  187 us (34%)
  local copies, waits for them, and re-layouts  84.6 us (15%)
  starting transfers between devices  44.9 us (8%)
  other arithmetic  12.7 us (2%)
    psum x1, blocking collectives, shards(): totals = lax.psum(jnp.sum(counts, axis=1), 'vocab')  220 us
    all_to_all x1, waiting for transfers between devices, shards(): lax.all_to_all(buckets, 'vocab', split_axis=0, concat_axis=0, tiled=True)  97 us
    all_to_all x1, waiting for transfers between devices, shards(): lax.all_to_all(first_rows, 'seq', split_axis=2, concat_axis=1, tiled=True)  89.8 us
    all_to_all x1, local copies, waits for them, and re-layouts, shards(): lax.all_to_all(buckets, 'vocab', split_axis=0, concat_axis=0, tiled=True)  21.6 us
    unnamed x6, local copies, waits for them, and re-layouts  21.6 us
    all_to_all x1, local copies, waits for them, and re-layouts, shards(): lax.all_to_all(first_rows, 'seq', split_axis=2, concat_axis=1, tiled=True)  21.1 us
    all_to_all x1, starting transfers between devices, shards(): lax.all_to_all(offset_tags, 'vocab', split_axis=0, concat_axis=0, tiled=T...  18.1 us
    all_to_all x1, starting transfers between devices, shards(): lax.all_to_all(buckets, 'vocab', split_axis=0, concat_axis=0, tiled=True)  15.4 us
  transfers between devices with their start and end apart: 4, of which 2 were waited for; matrix products, arithmetic and copies ran while one was open for 9% of the time, Pallas kernels for 0%

commit v1 on v0

v1 whole, which is shorter than its diff:
```python
import jax
import jax.numpy as jnp
from jax import lax
from jax.sharding import Mesh, PartitionSpec as P

VOCAB = 16384
SEQ = ("zlo", "core")
VOC = ("y", "x", "zhi")


def shards(posteriors, token_block, token_offset, lengths, smoothing):
    rows, states = posteriors.shape
    vocab_devs = lax.axis_size(VOC)
    seq_devs = lax.axis_size(SEQ)
    capacity = 2
    width = VOCAB // vocab_devs
    state_rows = states // seq_devs
    ratio = rows * vocab_devs * seq_devs / VOCAB
    me_v = lax.axis_index(VOC)
    me_s = lax.axis_index(SEQ)

    position = me_v * rows + jnp.arange(rows, dtype=jnp.int32)
    live = position < lengths[me_s]
    block = token_block[:, 0]
    same = (block[:, None] == block[None, :]) & live[None, :]
    row_ids = jnp.arange(rows, dtype=jnp.int32)
    rank = jnp.sum((same & (row_ids[None, :] < row_ids[:, None])).astype(jnp.int32), axis=1)
    slot = jnp.where(live, block * capacity + rank, -1)
    pick = (jnp.arange(vocab_devs * capacity, dtype=jnp.int32)[:, None] == slot[None, :]).astype(
        jnp.bfloat16
    )
    cube = posteriors.reshape(rows, seq_devs, state_rows)
    buckets = jnp.einsum("kr,rsn->skn", pick, cube, preferred_element_type=jnp.float32)
    buckets = buckets.astype(jnp.bfloat16).reshape(seq_devs * vocab_devs, capacity, state_rows)
    got = lax.all_to_all(buckets, SEQ + VOC, split_axis=0, concat_axis=0, tiled=True)

    part = jnp.dot(
        live.astype(jnp.bfloat16)[None, :], posteriors, preferred_element_type=jnp.float32
    )[0]
    tags = jnp.where(live, block * width + token_offset, -1).astype(jnp.float32)

    def place(values, axis):
        size = lax.axis_size(axis)
        hit = jnp.arange(size) == lax.axis_index(axis)
        return jnp.where(hit[:, None], values[None, :], 0.0).reshape(-1)

    joined = lax.psum(jnp.concatenate([part, place(tags, SEQ)]), SEQ)
    totals = lax.dynamic_slice(joined, (me_s * state_rows,), (state_rows,))
    tags = joined[states:]
    for axis in ("zhi", "x", "y"):
        joined = lax.psum(jnp.concatenate([totals, place(tags, axis)]), axis)
        totals, tags = joined[:state_rows], joined[state_rows:]
    tags = tags.astype(jnp.int32).reshape(vocab_devs, seq_devs, rows)
    tags = tags.transpose(1, 0, 2).reshape(vocab_devs * seq_devs, rows)
    big = rows * width
    keys = jnp.where(
        (tags >= me_v * width) & (tags < (me_v + 1) * width),
        row_ids[None, :] * width + tags - me_v * width,
        big,
    )
    first = jnp.min(keys, axis=1)
    second = jnp.min(jnp.where(keys > first[:, None], keys, big), axis=1)
    both = jnp.stack([first, second], axis=1)
    offset = jnp.where(both < big, both % width, -1).reshape(-1)

    one_hot = (offset[None, :] == jnp.arange(width, dtype=jnp.int32)[:, None]).astype(jnp.bfloat16)
    counts = jnp.dot(one_hot, got.reshape(-1, state_rows), preferred_element_type=jnp.float32)
    pseudo = smoothing * ratio
    emission = VOCAB * (counts + pseudo[None, :]) / (totals[None, :] + VOCAB * pseudo[None, :])
    return emission.T


def solution(mesh):
    fine = Mesh(mesh.devices.reshape(4, 2, 8, 4, 2), SEQ + VOC)
    placed = (P(SEQ + VOC, None), P(SEQ + VOC, None), P(SEQ + VOC), P(), P(SEQ))
    return jax.shard_map(
        shards, mesh=fine, in_specs=placed, out_specs=P(SEQ, VOC), check_vma=False
    )
```

time: 557 us -> 317 us (0.57)
  the two profiles are of different devices: /device:TPU:64 before, /device:TPU:1 now
where the time goes in v1:
time: 317 us; the launch traced here: 312 us
  waiting for transfers between devices  209 us (66%)
  blocking collectives  27.7 us (9%)
  starting transfers between devices  24.3 us (8%)
  local copies, waits for them, and re-layouts  18.4 us (6%)
  between operations  13.5 us (4%)
  matrix products  10.5 us (3%)
  other arithmetic  8.6 us (3%)
    psum x1, waiting for transfers between devices, shards(): joined = lax.psum(jnp.concatenate([part, place(tags, SEQ)]), SEQ)  136 us
    psum x1, waiting for transfers between devices, shards(): joined = lax.psum(jnp.concatenate([totals, place(tags, axis)]), axis)  73.4 us
    psum x2, blocking collectives, shards(): joined = lax.psum(jnp.concatenate([totals, place(tags, axis)]), axis)  27.7 us
    all_to_all x1, starting transfers between devices, shards(): lax.all_to_all(buckets, SEQ + VOC, split_axis=0, concat_axis=0, tiled=True)  24.2 us
    reshape x1, local copies, waits for them, and re-layouts, shards(): buckets.astype(jnp.bfloat16)  7.63 us
    reshape x1, local copies, waits for them, and re-layouts, shards(): got.reshape(-1, state_rows)  7.2 us
  transfers between devices with their start and end apart: 3, of which 2 were waited for; matrix products, arithmetic and copies ran while one was open for 3% of the time, Pallas kernels for 0%

profile of v1, /device:TPU:1, one launch (start us, length us, event | category | flops | bytes accessed | tf_op | source)
XLA Modules:
  0.0 312.0 jit_solution(15042151092838961881)
XLA Ops:
  6.5 1.2 dynamic_slice.6
  7.8 1.3 select_convert_fusion
  9.1 0.9 convert_reduce_fusion
  10.0 0.7 add_select_fusion.1
  10.7 4.9 %convert_bitcast_fusion = bf16[8,128,2048]{2,1,0:T(8,128)(2,1)} fusion(bf16[8,8,8,2048]{3,2,1,0:T(8,128)(2,1)} %bitcast.33, s32[64]{0:T(128)S(1)} %add_select_fusion.1), kind=kOutput, calls=%fused_computation | convolution fusion | flops 270540800 | bytes 6291712 | tf_op jit(solution)/shard_map/kr,rsn->skn/dot_general | solution.py:33
  15.6 7.6 %reshape.136 = bf16[512,2,2048]{2,1,0:T(2,128)(2,1)} reshape(bf16[8,128,2048]{2,1,0:T(8,128)(2,1)} %convert_bitcast_fusion) | data formatting | bytes 8388608 | tf_op jit(solution)/shard_map/reshape | solution.py:34
  23.2 0.0 copy-start
  23.2 24.2 %all-to-all-start = ((bf16[512,2,2048]{2,1,0:T(2,128)(2,1)}), bf16[512,2,2048]{2,1,0:T(2,128)(2,1)}, u32[]{:S(2)}, u32[]{:S(2)}) async-start(bf16[512,2,2048]{2,1,0:T(2,128)(2,1)} %reshape.136), calls=%async_computation | async-start | bytes 8388608 | tf_op jit(solution)/shard_map/all_to_all | solution.py:35
  47.4 0.0 all-reduce.3.cloned.1.call-start
  47.5 0.1 broadcast_select_fusion
  47.6 0.1 select_n.85
  47.6 0.0 copy-done
  47.6 0.4 fusion.12
  48.0 0.0 copy-start.1
  48.0 0.6 pad_maximum_fusion.1
  48.7 0.0 all-reduce.3.cloned.1.call-update
  48.7 0.0 all-reduce.5.cloned.1.call-start
  48.8 135.6 %all-reduce.3.cloned.1.call-done = f32[16896]{0:T(1024)} async-done(((f32[16896]{0:T(1024)}), f32[16896]{0:T(1024)}) %all-reduce.3.cloned.1.call-update) | async-done | bytes 67600 | tf_op jit(solution)/shard_map/psum | solution.py:47
  184.4 0.7 slice.36
  185.0 0.1 select_bitcast_fusion.2
  185.1 0.8 dynamic_slice.7
  185.9 14.5 %psum.29 = f32[3072]{0:T(1024)S(1)} all-reduce(f32[3072]{0:T(1024)S(1)} %pad_maximum_fusion.3), channel_id=1, replica_groups=mesh['zlo'=4,'core'=2,'y'=8,'x'=4,'zhi'=2] {'zhi'}, use_global_device_ids=true, to_apply=%region_2.3 | all-reduce | flops 3072 | bytes 24576 | tf_op jit(solution)/shard_map/psum | solution.py:51
  200.4 0.1 select_bitcast_fusion.1
  200.5 13.2 %psum.30 = f32[6144]{0:T(1024)S(1)} all-reduce(f32[6144]{0:T(1024)S(1)} %pad_maximum_fusion.2), channel_id=1, replica_groups=mesh['zlo'=4,'core'=2,'y'=8,'x'=4,'zhi'=2] {'x'}, use_global_device_ids=true, to_apply=%region_3.4 | all-reduce | flops 6144 | bytes 49152 | tf_op jit(solution)/shard_map/psum | solution.py:51
  213.7 0.1 select_bitcast_fusion
  213.8 0.7 pad_maximum_fusion
  214.5 0.0 all-reduce.5.cloned.1.call-update
  214.5 73.4 %all-reduce.5.cloned.1.call-done = f32[34816]{0:T(1024)} async-done(((f32[34816]{0:T(1024)}), f32[34816]{0:T(1024)}) %all-reduce.5.cloned.1.call-update) | async-done | bytes 139280 | tf_op jit(solution)/shard_map/psum | solution.py:51
  288.0 0.9 slice_convert_fusion
  288.9 0.1 convert_element_type.27
  289.0 1.2 bitcast_reduce_fusion
  290.1 0.1 copy.11
  290.2 1.2 fusion.5
  291.5 0.1 copy.12
  291.5 0.1 stack.12
  291.6 0.1 stack.11
  291.7 0.2 copy.13
  291.8 0.2 stack.14
  292.0 0.0 copy-done.1
  292.0 0.7 broadcast_multiply_fusion
  292.7 0.0 all-to-all-done
  292.8 7.2 %reshape.137 = bf16[1024,2048]{1,0:T(8,128)(2,1)} reshape(bf16[512,2,2048]{2,1,0:T(2,128)(2,1)} %all-to-all-done) | data formatting | bytes 8388608 | tf_op jit(solution)/shard_map/reshape | solution.py:67
  300.0 5.2 %fusion.1 = f32[2048,256]{1,0:T(8,128)} fusion(bf16[1024,2048]{1,0:T(8,128)(2,1)} %reshape.137, f32[2048]{0:T(1024)S(1)} %get-tuple-element.8, f32[2048]{0:T(1024)S(1)} %get-tuple-element.7, s32[1024]{0:T(1024)S(1)} %fusion.11), kind=kOutput, calls=%fused_computation.3 | convolution fusion | flops 1075576832 | bytes 6311936 | tf_op jit(solution)/shard_map/dot_general | solution.py:67
  (16 shorter events, 0.1 us)
Async XLA Ops:
  23.2 24.5 %copy-start = (bf16[64,16384]{1,0:T(8,128)(2,1)S(1)}, bf16[64,16384]{1,0:T(8,128)(2,1)}, u32[]{:S(2)}) copy-start(bf16[64,16384]{1,0:T(8,128)(2,1)} %param.5) | copy-start | bytes 6291460
  23.2 269.6 %all-to-all-start = ((bf16[512,2,2048]{2,1,0:T(2,128)(2,1)}), bf16[512,2,2048]{2,1,0:T(2,128)(2,1)}, u32[]{:S(2)}, u32[]{:S(2)}) async-start(bf16[512,2,2048]{2,1,0:T(2,128)(2,1)} %reshape.136), calls=%async_computation | async-start | bytes 8388608 | tf_op jit(solution)/shard_map/all_to_all | solution.py:35
  47.4 136.9 %all-reduce.3.cloned.1.call-start = ((), (), s32[]{:S(2)}) async-start(), calls=%async_computation.1 | async-start | bytes 139264 | tf_op jit(solution)/shard_map/psum | solution.py:47
  48.0 244.0 %copy-start.1 = (f32[2048]{0:T(1024)S(1)}, f32[2048]{0:T(1024)}, u32[]{:S(2)}) copy-start(f32[2048]{0:T(1024)} %param.9) | copy-start | bytes 24580
  48.7 239.3 %all-reduce.5.cloned.1.call-start = ((), (), s32[]{:S(2)}) async-start(), calls=%async_computation.2 | async-start | bytes 278528 | tf_op jit(solution)/shard_map/psum | solution.py:51
Sparse Core Ops, SparseCore 0:
  51.2 133.1 all-reduce.2
  214.6 73.2 all-reduce.4

commit v2 on v1

v2 whole, which is shorter than its diff:
```python
import jax
import jax.numpy as jnp
from jax import lax
from jax.sharding import Mesh, PartitionSpec as P

VOCAB = 16384
SEQ = ("z1", "z0", "core")
VOC = ("y2", "y1", "y0", "x1", "x0", "zhi")
LANES = 128


def swap(values, axis):
    return lax.ppermute(values, axis, [(0, 1), (1, 0)])


def small_exchange(part, table):
    seq_devs = lax.axis_size(SEQ)
    vocab_devs = table.shape[0]
    state_rows = part.shape[0] // seq_devs
    tot_rows = state_rows // LANES
    tags = jnp.broadcast_to(table[:, None, :], (vocab_devs, seq_devs, 2)).reshape(-1, LANES)
    tag_rows = tags.shape[0]
    index = lax.broadcasted_iota(jnp.int32, tags.shape, 0) * LANES + lax.broadcasted_iota(
        jnp.int32, tags.shape, 1
    )
    q = (index // 2) % seq_devs
    r = index // (2 * seq_devs)
    cur = part.reshape(seq_devs, tot_rows, LANES)
    for at, axis in reversed(list(enumerate(SEQ))):
        bit = lax.axis_index(axis)
        low = cur.reshape(-1, 2, tot_rows, LANES)
        keep = jnp.where(bit == 0, low[:, 0], low[:, 1])
        send = jnp.where(bit == 0, low[:, 1], low[:, 0])
        n = send.shape[0] * tot_rows
        got = swap(jnp.concatenate([send.reshape(n, LANES), tags]), axis)
        cur = keep + got[:n].reshape(keep.shape)
        side = (q >> (len(SEQ) - 1 - at)) & 1
        tags = jnp.where(side == 1, got[n:], tags)
    both = jnp.concatenate([cur.reshape(tot_rows, LANES), tags])
    pos = lax.broadcasted_iota(jnp.int32, both.shape, 0) * LANES + lax.broadcasted_iota(
        jnp.int32, both.shape, 1
    )
    rel = (pos - state_rows) // (2 * seq_devs)
    for at, axis in reversed(list(enumerate(VOC))):
        got = swap(both, axis)
        side = (rel >> (len(VOC) - 1 - at)) & 1
        both = jnp.where(pos < state_rows, both + got, jnp.where(side == 1, got, both))
    totals = both[:tot_rows].reshape(state_rows)
    tags = both[tot_rows:].reshape(vocab_devs, seq_devs * 2)
    return totals, tags


def absolute(tags, me_s, me_v):
    vocab_devs, width = tags.shape
    v = jnp.arange(vocab_devs)
    c = jnp.arange(width)
    left = ((v[:, None] ^ v[None, :]) == me_v).astype(jnp.bfloat16)
    right = ((c[:, None] ^ c[None, :]) == 2 * me_s).astype(jnp.bfloat16)
    tags = jnp.dot(left, tags.astype(jnp.bfloat16), preferred_element_type=jnp.float32)
    tags = jnp.dot(tags.astype(jnp.bfloat16), right, preferred_element_type=jnp.float32)
    tags = tags.reshape(vocab_devs, width // 2, 2)
    return tags.transpose(1, 0, 2).reshape(-1)


def shards(posteriors, token_block, token_offset, lengths, smoothing):
    rows, states = posteriors.shape
    vocab_devs = lax.axis_size(VOC)
    seq_devs = lax.axis_size(SEQ)
    capacity = 2
    width = VOCAB // vocab_devs
    state_rows = states // seq_devs
    ratio = rows * vocab_devs * seq_devs / VOCAB
    me_v = lax.axis_index(VOC)
    me_s = lax.axis_index(SEQ)

    position = me_v * rows + jnp.arange(rows, dtype=jnp.int32)
    live = position < lengths[me_s]
    block = token_block[:, 0]
    same = (block[:, None] == block[None, :]) & live[None, :]
    row_ids = jnp.arange(rows, dtype=jnp.int32)
    rank = jnp.sum((same & (row_ids[None, :] < row_ids[:, None])).astype(jnp.int32), axis=1)
    slot = jnp.where(live, block * capacity + rank, -1)
    slots = jnp.arange(vocab_devs * capacity, dtype=jnp.int32)
    pick = (slots[:, None] == slot[None, :]).astype(jnp.bfloat16)
    cube = posteriors.reshape(rows, seq_devs, state_rows)
    buckets = jnp.einsum("kr,rsn->skn", pick, cube, preferred_element_type=jnp.float32)
    buckets = buckets.astype(jnp.bfloat16).reshape(seq_devs * vocab_devs, capacity, state_rows)
    got = lax.all_to_all(buckets, SEQ + VOC, split_axis=0, concat_axis=0, tiled=True)

    part = jnp.dot(
        live.astype(jnp.bfloat16)[None, :], posteriors, preferred_element_type=jnp.float32
    )[0]
    rel_hit = (slots ^ (2 * me_v))[:, None] == slot[None, :]
    table = jnp.sum(jnp.where(rel_hit, token_offset[None, :] + 1, 0), axis=1) - 1
    table = table.astype(jnp.float32).reshape(vocab_devs, capacity)
    totals, tags = small_exchange(part, table)
    offset = absolute(tags, me_s, me_v)

    one_hot = (
        offset[None, :] == jnp.arange(width, dtype=jnp.int32)[:, None].astype(jnp.float32)
    ).astype(jnp.bfloat16)
    counts = jnp.dot(one_hot, got.reshape(-1, state_rows), preferred_element_type=jnp.float32)
    pseudo = smoothing * ratio
    emission = VOCAB * (counts + pseudo[None, :]) / (totals[None, :] + VOCAB * pseudo[None, :])
    return emission.T


def solution(mesh):
    fine = Mesh(mesh.devices.reshape((2,) * (len(SEQ) + len(VOC))), SEQ + VOC)
    placed = (P(SEQ + VOC, None), P(SEQ + VOC, None), P(SEQ + VOC), P(), P(SEQ))
    return jax.shard_map(
        shards, mesh=fine, in_specs=placed, out_specs=P(SEQ, VOC), check_vma=False
    )
```

time: 317 us -> 198 us (0.62)
  the two profiles are of different devices: /device:TPU:1 before, /device:TPU:78 now
where the time goes in v2:
time: 198 us
  waiting for transfers between devices  96.9 us (49%)
  starting transfers between devices  67.4 us (34%)
  local copies, waits for them, and re-layouts  17.5 us (9%)
  matrix products  11.7 us (6%)
  other arithmetic  3.85 us (2%)
    ppermute x9, waiting for transfers between devices, swap(): return lax.ppermute(values, axis, [(0, 1), (1, 0)])  96.9 us
    ppermute x9, starting transfers between devices, swap(): return lax.ppermute(values, axis, [(0, 1), (1, 0)])  44.7 us
    all_to_all x1, starting transfers between devices, shards(): lax.all_to_all(buckets, SEQ + VOC, split_axis=0, concat_axis=0, tiled=True)  22.7 us
    reshape x1, local copies, waits for them, and re-layouts, shards(): buckets.astype(jnp.bfloat16)  7.68 us
    reshape x1, local copies, waits for them, and re-layouts, shards(): got.reshape(-1, state_rows)  7.28 us
    dot_general x1, matrix products, shards(): jnp.dot(one_hot, got.reshape(-1, state_rows), preferred_element_type=jnp....  5.27 us
    dot_general x1, matrix products, shards(): jnp.einsum('kr,rsn->skn', pick, cube, preferred_element_type=jnp.float32)  4.9 us
  transfers between devices with their start and end apart: 10, of which 9 were waited for; matrix products, arithmetic and copies ran while one was open for 2% of the time, Pallas kernels for 0%

profile of v2, /device:TPU:78, one launch (start us, length us, event | category | flops | bytes accessed | tf_op | source)
XLA Modules:
  0.0 197.7 jit_solution(2223238151360289362)
XLA Ops:
  0.0 1.2 dynamic_slice.3
  1.2 0.7 add_compare_fusion
  1.9 0.9 convert_reduce_fusion
  2.8 1.3 add_select_fusion.3
  4.1 4.9 %convert_bitcast_fusion = bf16[8,128,2048]{2,1,0:T(8,128)(2,1)} fusion(bf16[8,8,8,2048]{3,2,1,0:T(8,128)(2,1)} %bitcast.45, s32[64]{0:T(128)S(1)} %get-tuple-element.9), kind=kOutput, calls=%fused_computation | convolution fusion | flops 270540800 | bytes 6291712 | tf_op jit(solution)/shard_map/kr,rsn->skn/dot_general | solution.py:86
  9.0 7.7 %reshape.139 = bf16[512,2,2048]{2,1,0:T(2,128)(2,1)} reshape(bf16[8,128,2048]{2,1,0:T(8,128)(2,1)} %convert_bitcast_fusion) | data formatting | bytes 8388608 | tf_op jit(solution)/shard_map/reshape | solution.py:87
  16.7 0.0 copy-start
  16.7 22.7 %all-to-all-start = ((bf16[512,2,2048]{2,1,0:T(2,128)(2,1)}), bf16[512,2,2048]{2,1,0:T(2,128)(2,1)}, u32[]{:S(2)}, u32[]{:S(2)}) async-start(bf16[512,2,2048]{2,1,0:T(2,128)(2,1)} %reshape.139), calls=%async_computation | async-start | bytes 8388608 | tf_op jit(solution)/shard_map/all_to_all | solution.py:88
  39.4 0.1 select_reduce_fusion
  39.6 0.1 convert_element_type.43
  39.7 0.2 reshape.141
  39.9 0.0 copy-done
  39.9 0.6 copy.16
  40.5 0.0 copy-start.1
  40.5 1.2 fusion.4
  41.7 2.1 %collective-permute-start = (f32[72,128]{1,0:T(8,128)S(1)}, f32[72,128]{1,0:T(8,128)S(1)}, u32[]{:S(2)}, u32[]{:S(2)}) collective-permute-start(f32[72,128]{1,0:T(8,128)S(1)} %pad_maximum_fusion), channel_id=1, source_target_pairs={{0,64},{64,0},{1,65},{65,1},{2,66},{66,2},{3,67},{67,3},{4,68},{68... | collective-permute-start | bytes 110600 | tf_op jit(solution)/shard_map/ppermute | solution.py:13
  43.8 1.0 collective-permute-done
  44.9 0.1 slice_select_fusion.5
  45.0 2.0 collective-permute-start.1
  47.0 68.1 %collective-permute-done.1 = f32[40,128]{1,0:T(8,128)S(1)} collective-permute-done((f32[40,128]{1,0:T(8,128)S(1)}, f32[40,128]{1,0:T(8,128)S(1)}, u32[]{:S(2)}, u32[]{:S(2)}) %collective-permute-start.1) | collective-permute-done | bytes 20512 | tf_op jit(solution)/shard_map/ppermute | solution.py:13
  115.0 0.1 slice_select_fusion.4
  115.2 15.8 %collective-permute-start.2 = (f32[24,128]{1,0:T(8,128)S(1)}, f32[24,128]{1,0:T(8,128)S(1)}, u32[]{:S(2)}, u32[]{:S(2)}) collective-permute-start(f32[24,128]{1,0:T(8,128)S(1)} %pad_maximum_fusion.2), channel_id=1, source_target_pairs={{0,256},{256,0},{1,257},{257,1},{2,258},{258,2},{3,259},{259,3},{4... | collective-permute-start | bytes 36872 | tf_op jit(solution)/shard_map/ppermute | solution.py:13
  131.0 1.8 collective-permute-done.2
  132.8 0.1 slice_select_fusion.3
  132.9 15.0 %collective-permute-start.3 = (f32[24,128]{1,0:T(8,128)S(1)}, f32[24,128]{1,0:T(8,128)S(1)}, u32[]{:S(2)}, u32[]{:S(2)}) collective-permute-start(f32[24,128]{1,0:T(8,128)S(1)} %pad_maximum_fusion.3), channel_id=1, source_target_pairs={{0,1},{1,0},{2,3},{3,2},{4,5},{5,4},{6,7},{7,6},{8,9},{9,8},{10,11... | collective-permute-start | bytes 36872 | tf_op jit(solution)/shard_map/ppermute | solution.py:13
  147.9 1.6 collective-permute-done.3
  149.6 0.1 select_select_fusion.5
  149.6 1.9 collective-permute-start.4
  151.6 3.7 %collective-permute-done.4 = f32[24,128]{1,0:T(8,128)S(1)} collective-permute-done((f32[24,128]{1,0:T(8,128)S(1)}, f32[24,128]{1,0:T(8,128)S(1)}, u32[]{:S(2)}, u32[]{:S(2)}) %collective-permute-start.4) | collective-permute-done | bytes 12320 | tf_op jit(solution)/shard_map/ppermute | solution.py:13
  155.2 0.1 select_select_fusion.4
  155.3 2.1 %collective-permute-start.5 = (f32[24,128]{1,0:T(8,128)S(1)}, f32[24,128]{1,0:T(8,128)S(1)}, u32[]{:S(2)}, u32[]{:S(2)}) collective-permute-start(f32[24,128]{1,0:T(8,128)S(1)} %select_select_fusion.4), channel_id=1, source_target_pairs={{0,4},{4,0},{1,5},{5,1},{2,6},{6,2},{3,7},{7,3},{8,12},{12,8},{9,1... | collective-permute-start | bytes 36872 | tf_op jit(solution)/shard_map/ppermute | solution.py:13
  157.4 5.0 %collective-permute-done.5 = f32[24,128]{1,0:T(8,128)S(1)} collective-permute-done((f32[24,128]{1,0:T(8,128)S(1)}, f32[24,128]{1,0:T(8,128)S(1)}, u32[]{:S(2)}, u32[]{:S(2)}) %collective-permute-start.5) | collective-permute-done | bytes 12320 | tf_op jit(solution)/shard_map/ppermute | solution.py:13
  162.4 0.1 select_select_fusion.3
  162.5 1.9 collective-permute-start.6
  164.4 3.7 %collective-permute-done.6 = f32[24,128]{1,0:T(8,128)S(1)} collective-permute-done((f32[24,128]{1,0:T(8,128)S(1)}, f32[24,128]{1,0:T(8,128)S(1)}, u32[]{:S(2)}, u32[]{:S(2)}) %collective-permute-start.6) | collective-permute-done | bytes 12320 | tf_op jit(solution)/shard_map/ppermute | solution.py:13
  168.1 0.1 select_select_fusion.2
  168.2 1.9 collective-permute-start.7
  170.1 4.6 %collective-permute-done.7 = f32[24,128]{1,0:T(8,128)S(1)} collective-permute-done((f32[24,128]{1,0:T(8,128)S(1)}, f32[24,128]{1,0:T(8,128)S(1)}, u32[]{:S(2)}, u32[]{:S(2)}) %collective-permute-start.7) | collective-permute-done | bytes 12320 | tf_op jit(solution)/shard_map/ppermute | solution.py:13
  174.7 0.1 select_select_fusion.1
  174.8 2.1 %collective-permute-start.8 = (f32[24,128]{1,0:T(8,128)S(1)}, f32[24,128]{1,0:T(8,128)S(1)}, u32[]{:S(2)}, u32[]{:S(2)}) collective-permute-start(f32[24,128]{1,0:T(8,128)S(1)} %select_select_fusion.1), channel_id=1, source_target_pairs={{0,32},{32,0},{1,33},{33,1},{2,34},{34,2},{3,35},{35,3},{4,36},{36... | collective-permute-start | bytes 36872 | tf_op jit(solution)/shard_map/ppermute | solution.py:13
  176.9 7.4 %collective-permute-done.8 = f32[24,128]{1,0:T(8,128)S(1)} collective-permute-done((f32[24,128]{1,0:T(8,128)S(1)}, f32[24,128]{1,0:T(8,128)S(1)}, u32[]{:S(2)}, u32[]{:S(2)}) %collective-permute-start.8) | collective-permute-done | bytes 12320 | tf_op jit(solution)/shard_map/ppermute | solution.py:13
  184.3 0.1 select_select_fusion
  184.4 0.1 convert_element_type.44
  184.4 0.3 fusion.6
  184.7 0.2 copy.11
  184.9 0.2 eq.129
  185.1 0.0 copy-done.1
  185.1 0.0 all-to-all-done
  185.1 7.3 %reshape.140 = bf16[1024,2048]{1,0:T(8,128)(2,1)} reshape(bf16[512,2,2048]{2,1,0:T(2,128)(2,1)} %all-to-all-done) | data formatting | bytes 8388608 | tf_op jit(solution)/shard_map/reshape | solution.py:102
  192.4 5.3 %fusion.1 = f32[2048,256]{1,0:T(8,128)} fusion(bf16[1024,2048]{1,0:T(8,128)(2,1)} %reshape.140, f32[2048]{0:T(1024)S(1)} %get-tuple-element.8, f32[2048]{0:T(1024)S(1)} %get-tuple-element.7, f32[1024]{0:T(1024)S(1)} %eq.129, f32[256]{0:T(256)S(1)} %iota_convert_fusion), kind=kOutput, calls=%fused_computation.3 | convolution fusion | flops 1075576832 | bytes 6312960 | tf_op jit(solution)/shard_map/dot_general | solution.py:102
  (21 shorter events, 0.1 us)
Async XLA Ops:
  16.7 23.2 %copy-start = (bf16[64,16384]{1,0:T(8,128)(2,1)S(1)}, bf16[64,16384]{1,0:T(8,128)(2,1)}, u32[]{:S(2)}) copy-start(bf16[64,16384]{1,0:T(8,128)(2,1)} %param.5) | copy-start | bytes 6291460
  16.7 168.4 %all-to-all-start = ((bf16[512,2,2048]{2,1,0:T(2,128)(2,1)}), bf16[512,2,2048]{2,1,0:T(2,128)(2,1)}, u32[]{:S(2)}, u32[]{:S(2)}) async-start(bf16[512,2,2048]{2,1,0:T(2,128)(2,1)} %reshape.139), calls=%async_computation | async-start | bytes 8388608 | tf_op jit(solution)/shard_map/all_to_all | solution.py:88
  40.5 144.6 %copy-start.1 = (f32[2048]{0:T(1024)S(1)}, f32[2048]{0:T(1024)}, u32[]{:S(2)}) copy-start(f32[2048]{0:T(1024)} %param.9) | copy-start | bytes 24580
  41.7 3.1 %collective-permute-start = (f32[72,128]{1,0:T(8,128)S(1)}, f32[72,128]{1,0:T(8,128)S(1)}, u32[]{:S(2)}, u32[]{:S(2)}) collective-permute-start(f32[72,128]{1,0:T(8,128)S(1)} %pad_maximum_fusion), channel_id=1, source_target_pairs={{0,64},{64,0},{1,65},{65,1},{2,66},{66,2},{3,67},{67,3},{4,68},{68... | collective-permute-start | bytes 110600 | tf_op jit(solution)/shard_map/ppermute | solution.py:13
  45.0 70.1 %collective-permute-start.1 = (f32[40,128]{1,0:T(8,128)S(1)}, f32[40,128]{1,0:T(8,128)S(1)}, u32[]{:S(2)}, u32[]{:S(2)}) collective-permute-start(f32[40,128]{1,0:T(8,128)S(1)} %pad_maximum_fusion.1), channel_id=1, source_target_pairs={{0,128},{128,0},{1,129},{129,1},{2,130},{130,2},{3,131},{131,3},{4... | collective-permute-start | bytes 61448 | tf_op jit(solution)/shard_map/ppermute | solution.py:13
  115.2 17.7 %collective-permute-start.2 = (f32[24,128]{1,0:T(8,128)S(1)}, f32[24,128]{1,0:T(8,128)S(1)}, u32[]{:S(2)}, u32[]{:S(2)}) collective-permute-start(f32[24,128]{1,0:T(8,128)S(1)} %pad_maximum_fusion.2), channel_id=1, source_target_pairs={{0,256},{256,0},{1,257},{257,1},{2,258},{258,2},{3,259},{259,3},{4... | collective-permute-start | bytes 36872 | tf_op jit(solution)/shard_map/ppermute | solution.py:13
  132.9 16.6 %collective-permute-start.3 = (f32[24,128]{1,0:T(8,128)S(1)}, f32[24,128]{1,0:T(8,128)S(1)}, u32[]{:S(2)}, u32[]{:S(2)}) collective-permute-start(f32[24,128]{1,0:T(8,128)S(1)} %pad_maximum_fusion.3), channel_id=1, source_target_pairs={{0,1},{1,0},{2,3},{3,2},{4,5},{5,4},{6,7},{7,6},{8,9},{9,8},{10,11... | collective-permute-start | bytes 36872 | tf_op jit(solution)/shard_map/ppermute | solution.py:13
  149.6 5.6 %collective-permute-start.4 = (f32[24,128]{1,0:T(8,128)S(1)}, f32[24,128]{1,0:T(8,128)S(1)}, u32[]{:S(2)}, u32[]{:S(2)}) collective-permute-start(f32[24,128]{1,0:T(8,128)S(1)} %select_select_fusion.5), channel_id=1, source_target_pairs={{0,2},{2,0},{1,3},{3,1},{4,6},{6,4},{5,7},{7,5},{8,10},{10,8},{9,1... | collective-permute-start | bytes 36872 | tf_op jit(solution)/shard_map/ppermute | solution.py:13
  155.3 7.1 %collective-permute-start.5 = (f32[24,128]{1,0:T(8,128)S(1)}, f32[24,128]{1,0:T(8,128)S(1)}, u32[]{:S(2)}, u32[]{:S(2)}) collective-permute-start(f32[24,128]{1,0:T(8,128)S(1)} %select_select_fusion.4), channel_id=1, source_target_pairs={{0,4},{4,0},{1,5},{5,1},{2,6},{6,2},{3,7},{7,3},{8,12},{12,8},{9,1... | collective-permute-start | bytes 36872 | tf_op jit(solution)/shard_map/ppermute | solution.py:13
  162.5 5.6 %collective-permute-start.6 = (f32[24,128]{1,0:T(8,128)S(1)}, f32[24,128]{1,0:T(8,128)S(1)}, u32[]{:S(2)}, u32[]{:S(2)}) collective-permute-start(f32[24,128]{1,0:T(8,128)S(1)} %select_select_fusion.3), channel_id=1, source_target_pairs={{0,8},{8,0},{1,9},{9,1},{2,10},{10,2},{3,11},{11,3},{4,12},{12,4},... | collective-permute-start | bytes 36872 | tf_op jit(solution)/shard_map/ppermute | solution.py:13
  168.2 6.5 %collective-permute-start.7 = (f32[24,128]{1,0:T(8,128)S(1)}, f32[24,128]{1,0:T(8,128)S(1)}, u32[]{:S(2)}, u32[]{:S(2)}) collective-permute-start(f32[24,128]{1,0:T(8,128)S(1)} %select_select_fusion.2), channel_id=1, source_target_pairs={{0,16},{16,0},{1,17},{17,1},{2,18},{18,2},{3,19},{19,3},{4,20},{20... | collective-permute-start | bytes 36872 | tf_op jit(solution)/shard_map/ppermute | solution.py:13
  174.8 9.5 %collective-permute-start.8 = (f32[24,128]{1,0:T(8,128)S(1)}, f32[24,128]{1,0:T(8,128)S(1)}, u32[]{:S(2)}, u32[]{:S(2)}) collective-permute-start(f32[24,128]{1,0:T(8,128)S(1)} %select_select_fusion.1), channel_id=1, source_target_pairs={{0,32},{32,0},{1,33},{33,1},{2,34},{34,2},{3,35},{35,3},{4,36},{36... | collective-permute-start | bytes 36872 | tf_op jit(solution)/shard_map/ppermute | solution.py:13

commit v3 on v1

v3 whole, which is shorter than its diff:
```python
import functools

import jax
import jax.numpy as jnp
from jax import lax
from jax.experimental import pallas as pl
from jax.experimental.pallas import tpu as pltpu
from jax.sharding import Mesh, PartitionSpec as P

VOCAB = 16384
SEQ = ("zlo", "core")
VOC = ("y", "x", "zhi")
TEAM = ("zlo", "core", "x")
LANES = 128
CAP = 2
HALF = 64
F32 = jnp.float32
BF16 = jnp.bfloat16
VMEM_LIMIT = 60 * 2**20


def live_rows(rows, lengths_ref):
    bound = lengths_ref[lax.axis_index(SEQ)] - lax.axis_index(VOC) * rows
    return lambda shape, dim: lax.broadcasted_iota(jnp.int32, shape, dim) < bound


def part_kernel(rows, seq_devs, slice_rows, lengths_ref, x_ref, o_ref, acc_ref):
    s = pl.program_id(0)
    shape = (seq_devs, rows)
    live = live_rows(rows, lengths_ref)(shape, 1)
    mine = lax.broadcasted_iota(jnp.int32, shape, 0) == s
    left = jnp.where(live & mine, 1.0, 0.0).astype(BF16)
    term = jnp.dot(left, x_ref[...], preferred_element_type=F32)

    @pl.when(s == 0)
    def _():
        acc_ref[...] = term

    @pl.when(s > 0)
    def _():
        acc_ref[...] += term

    @pl.when(s == seq_devs - 1)
    def _():
        for t in range(slice_rows // LANES):
            tile = acc_ref[:, t * LANES : (t + 1) * LANES]
            o_ref[2 * t] = tile
            o_ref[2 * t + 1] = pltpu.roll(tile, HALF, 1)


def bucket_kernel(rows, slots, lengths_ref, blk_ref, off_ref, x_ref, o_ref, tag_ref, pick_ref):
    slice_rows = x_ref.shape[1]

    @pl.when(pl.program_id(0) == 0)
    def _():
        shape = (slots, rows)
        live = live_rows(rows, lengths_ref)(shape, 1)
        k = lax.broadcasted_iota(jnp.int32, shape, 0)
        hit = live & (blk_ref[...] == k // CAP)
        before = lax.broadcasted_iota(jnp.int32, (rows, rows), 0) < lax.broadcasted_iota(
            jnp.int32, (rows, rows), 1
        )
        rank = jnp.dot(
            jnp.where(hit, 1.0, 0.0).astype(BF16),
            jnp.where(before, 1.0, 0.0).astype(BF16),
            preferred_element_type=F32,
        )
        pick = hit & (rank == (k % CAP).astype(F32))
        pick_ref[...] = jnp.where(pick, 1.0, 0.0).astype(BF16)
        value = jnp.where(pick, (off_ref[...] + 1).astype(F32), 0.0)
        tag = jnp.sum(value, axis=1, keepdims=True) - 1.0
        lane = lax.broadcasted_iota(jnp.int32, (slots, LANES), 1)
        tag_ref[...] = jnp.where(lane == HALF, tag, 0.0)

    y = jnp.dot(pick_ref[...], x_ref[...], preferred_element_type=F32).astype(BF16)
    o_ref[:, :, :slice_rows] = y.reshape(slots // CAP, CAP, slice_rows)
    o_ref[:, :, slice_rows:] = jnp.zeros((slots // CAP, CAP, LANES), BF16)


def carry_kernel(seq_devs, slots, sums_ref, tag_ref, send_ref, o_ref):
    del send_ref
    total = jnp.sum(sums_ref[...], axis=0)
    high = total.astype(BF16).astype(F32)
    low = total - high
    shape = (slots, LANES)
    odd = lax.broadcasted_iota(jnp.int32, shape, 0) % CAP == 1
    lane = lax.broadcasted_iota(jnp.int32, shape, 1)
    tag = tag_ref[...]
    n = slots // CAP
    for s in range(seq_devs):
        both = jnp.where(odd, low[s : s + 1], high[s : s + 1])
        carry = jnp.where(lane < HALF, both, tag).astype(BF16)
        o_ref[s * n : (s + 1) * n] = carry.reshape(n, CAP, LANES)


def final_kernel(dims, ratio, smooth_ref, data_ref, carry_ref, o_ref, hot_ref, tot_ref):
    seq_devs, y_devs, x_devs, h_devs = dims
    p = pl.program_id(0)
    kk = seq_devs * y_devs * x_devs * h_devs * CAP
    width = o_ref.shape[1]
    cols = data_ref.shape[2]
    tiles = cols // LANES

    @pl.when(p == 0)
    def _():
        carry = carry_ref[...].reshape(kk, LANES)
        sel = lax.broadcasted_iota(jnp.int32, (16, LANES), 1) == HALF
        off = lax.dot_general(
            jnp.where(sel, 1.0, 0.0).astype(BF16),
            carry,
            (((1,), (1,)), ((), ())),
            preferred_element_type=F32,
        )[0:1]
        v = lax.broadcasted_iota(jnp.int32, (width, kk), 0).astype(F32)
        hot_ref[...] = jnp.where(off == v, 1.0, 0.0).astype(BF16)
        n = tot_ref.shape[0]
        k = lax.broadcasted_iota(jnp.int32, (n, kk), 1)
        member = (k // (kk // seq_devs)) * x_devs + (k // (CAP * h_devs)) % x_devs
        t = lax.broadcasted_iota(jnp.int32, (n, kk), 0)
        even = jnp.where(member == 2 * t, 1.0, 0.0).astype(BF16)
        odd = jnp.where(member == 2 * t + 1, 1.0, 0.0).astype(BF16)
        even = jnp.dot(even, carry, preferred_element_type=F32)
        odd = jnp.dot(odd, carry, preferred_element_type=F32)
        lane = lax.broadcasted_iota(jnp.int32, (n, LANES), 1)
        tot_ref[...] = jnp.where(lane < HALF, even, pltpu.roll(odd, HALF, 1))

    counts = jnp.dot(hot_ref[...], data_ref[...].reshape(kk, cols), preferred_element_type=F32)
    for i in range(tiles):
        pseudo = smooth_ref[pl.ds(p * tiles + i, 1), :] * ratio
        scale = VOCAB / (tot_ref[pl.ds(p * tiles + i, 1), :] + VOCAB * pseudo)
        done = (counts[:, i * LANES : (i + 1) * LANES] + pseudo) * scale
        o_ref[i * LANES : (i + 1) * LANES, :] = done.T


def shards(posteriors, token_block, token_offset, lengths, smoothing):
    rows, states = posteriors.shape
    seq_devs = lax.axis_size(SEQ)
    vocab_devs = lax.axis_size(VOC)
    devs = seq_devs * vocab_devs
    team = lax.axis_size(TEAM)
    width = VOCAB // vocab_devs
    slice_rows = states // seq_devs
    slots = vocab_devs * CAP
    chunk = slice_rows + LANES
    ratio = rows * devs / VOCAB
    params = pltpu.CompilerParams(vmem_limit_bytes=VMEM_LIMIT)
    smem = pl.BlockSpec(memory_space=pltpu.SMEM)
    x_spec = pl.BlockSpec((rows, slice_rows), lambda s: (0, s))

    part = pl.pallas_call(
        functools.partial(part_kernel, rows, seq_devs, slice_rows),
        grid=(seq_devs,),
        in_specs=[smem, x_spec],
        out_specs=pl.BlockSpec((team, seq_devs, LANES), lambda s: (0, 0, 0)),
        out_shape=jax.ShapeDtypeStruct((team, seq_devs, LANES), F32),
        scratch_shapes=[pltpu.VMEM((seq_devs, slice_rows), F32)],
        compiler_params=params,
        name="part",
    )(lengths, posteriors)
    sums = lax.all_to_all(part, TEAM, split_axis=0, concat_axis=0, tiled=True)

    row_spec = pl.BlockSpec((1, rows), lambda s: (0, 0))
    send, tag = pl.pallas_call(
        functools.partial(bucket_kernel, rows, slots),
        grid=(seq_devs,),
        in_specs=[smem, row_spec, row_spec, x_spec],
        out_specs=[
            pl.BlockSpec((vocab_devs, CAP, chunk), lambda s: (s, 0, 0)),
            pl.BlockSpec((slots, LANES), lambda s: (0, 0)),
        ],
        out_shape=[
            jax.ShapeDtypeStruct((devs, CAP, chunk), BF16),
            jax.ShapeDtypeStruct((slots, LANES), F32),
        ],
        scratch_shapes=[pltpu.VMEM((slots, rows), BF16)],
        compiler_params=params,
        cost_estimate=pl.CostEstimate(
            flops=2 * slots * rows * states, bytes_accessed=8 * rows * states, transcendentals=0
        ),
        name="bucket",
    )(lengths, token_block.reshape(1, rows), token_offset.reshape(1, rows), posteriors)

    tail = slice_rows // LANES
    send = pl.pallas_call(
        functools.partial(carry_kernel, seq_devs, slots),
        grid=(1,),
        in_specs=[
            pl.BlockSpec((team, seq_devs, LANES), lambda i: (0, 0, 0)),
            pl.BlockSpec((slots, LANES), lambda i: (0, 0)),
            pl.BlockSpec(memory_space=pl.ANY),
        ],
        out_specs=pl.BlockSpec((devs, CAP, LANES), lambda i: (0, 0, tail)),
        out_shape=jax.ShapeDtypeStruct((devs, CAP, chunk), BF16),
        input_output_aliases={2: 0},
        compiler_params=params,
        name="carry",
    )(sums, tag, send)

    got = lax.all_to_all(send, SEQ + VOC, split_axis=0, concat_axis=0, tiled=True)

    cols = 2 * LANES
    dims = (seq_devs,) + tuple(lax.axis_size(a) for a in VOC)
    return pl.pallas_call(
        functools.partial(final_kernel, dims, ratio),
        grid=(slice_rows // cols,),
        in_specs=[
            pl.BlockSpec((tail, LANES), lambda p: (0, 0)),
            pl.BlockSpec((devs, CAP, cols), lambda p: (0, 0, p)),
            pl.BlockSpec((devs, CAP, LANES), lambda p: (0, 0, tail)),
        ],
        out_specs=pl.BlockSpec((cols, width), lambda p: (p, 0)),
        out_shape=jax.ShapeDtypeStruct((slice_rows, width), F32),
        scratch_shapes=[
            pltpu.VMEM((width, devs * CAP), BF16),
            pltpu.VMEM((tail, LANES), F32),
        ],
        compiler_params=params,
        name="final",
    )(smoothing.reshape(tail, LANES), got, got)


def solution(mesh):
    fine = Mesh(mesh.devices.reshape(4, 2, 8, 4, 2), SEQ + VOC)
    placed = (P(SEQ + VOC, None), P(SEQ + VOC, None), P(SEQ + VOC), P(), P(SEQ))
    return jax.shard_map(
        shards, mesh=fine, in_specs=placed, out_specs=P(SEQ, VOC), check_vma=False
    )
```

time: 317 us -> 164 us (0.52)
  the two profiles are of different devices: /device:TPU:1 before, /device:TPU:8 now
where the time goes in v3:
time: 164 us; the launch traced here: 163 us
  blocking collectives  128 us (78%)
  Pallas kernels  23 us (14%)
  starting transfers between devices  10.1 us (6%)
    all_to_all x1, blocking collectives, shards(): lax.all_to_all(send, SEQ + VOC, split_axis=0, concat_axis=0, tiled=True)  128 us
    all_to_all x1, starting transfers between devices, shards(): sums = lax.all_to_all(part, TEAM, split_axis=0, concat_axis=0, tiled=True)  10.1 us
    pallas_call x1, Pallas kernels, shards(): pl.pallas_call(functools.partial(final_kernel, dims, ratio), grid=(slice_...  8.32 us
    pallas_call x1, Pallas kernels, shards(): pl.pallas_call(functools.partial(bucket_kernel, rows, slots), grid=(seq_d...  7.34 us
    pallas_call x1, Pallas kernels, shards(): pl.pallas_call(functools.partial(part_kernel, rows, seq_devs, slice_rows)...  5.52 us
  transfers between devices with their start and end apart: 1, of which 1 were waited for; matrix products, arithmetic and copies ran while one was open for 0% of the time, Pallas kernels for 4%

profile of v3, /device:TPU:8, one launch (start us, length us, event | category | flops | bytes accessed | tf_op | source)
XLA Modules:
  0.0 163.2 jit_solution(6885911082015854160)
XLA Ops:
  0.0 5.5 %part.1 = f32[32,8,128]{2,1,0:T(8,128)} custom-call(s32[8]{0:T(128)} %lengths_ref.3, bf16[64,16384]{1,0:T(8,128)(2,1)} %x_ref.3), custom_call_target="tpu_custom_call" | custom-call | tf_op jit(solution)/shard_map/part/pallas_call | solution.py:150
  5.5 10.1 %all-to-all-start = ((f32[32,8,128]{2,1,0:T(8,128)}), f32[32,8,128]{2,1,0:T(8,128)S(1)}, u32[]{:S(2)}, u32[]{:S(2)}) async-start(f32[32,8,128]{2,1,0:T(8,128)} %part.1), calls=%async_computation | async-start | bytes 262144 | tf_op jit(solution)/shard_map/all_to_all | solution.py:160
  15.6 7.3 %bucket.1 = (bf16[512,2,2176]{2,1,0:T(2,128)(2,1)}, f32[128,128]{1,0:T(8,128)}) custom-call(s32[8]{0:T(128)} %lengths_ref.3, s32[1,64]{1,0:T(1,128)} %bitcast.4, s32[1,64]{1,0:T(1,128)} %bitcast.5, bf16[64,16384]{1,0:T(8,128)(2,1)} %x_ref.3), custom_call_target="tpu_custom_call" | custom-call | flops 268435456 | bytes 8388608 | tf_op jit(solution)/shard_map/bucket/pallas_call | solution.py:163
  23.0 1.4 all-to-all-done.sums_ref
  24.4 0.0 copy-start
  24.4 0.7 copy-done
  25.0 1.8 %carry.1 = bf16[512,2,2176]{2,1,0:T(2,128)(2,1)} custom-call(f32[32,8,128]{2,1,0:T(8,128)} %copy-done, f32[128,128]{1,0:T(8,128)} %get-tuple-element.7.tag_ref, bf16[512,2,2176]{2,1,0:T(2,128)(2,1)} %get-tuple-element.8.send_ref), custom_call_target="tpu_custom_call", output_to_operand_aliasing={{}: (2, {})} | custom-call | tf_op jit(solution)/shard_map/carry/pallas_call | solution.py:184
  26.9 128.0 %all_to_all.10.data_ref.carry_ref = bf16[512,2,2176]{2,1,0:T(2,128)(2,1)} all-to-all(bf16[512,2,2176]{2,1,0:T(2,128)(2,1)} %carry.1), channel_id=1, replica_groups=mesh['zlo'=4,'core'=2,'y'=8,'x'=4,'zhi'=2] {'zlo','core','y','x','zhi'}, dimensions={0} | all-to-all | bytes 8912896 | tf_op jit(solution)/shard_map/all_to_all | solution.py:199
  154.9 8.3 %final.1 = f32[2048,256]{1,0:T(8,128)} custom-call(f32[16,128]{1,0:T(8,128)} %bitcast.3, bf16[512,2,2176]{2,1,0:T(2,128)(2,1)} %all_to_all.10.data_ref.carry_ref, bf16[512,2,2176]{2,1,0:T(2,128)(2,1)} %all_to_all.10.data_ref.carry_ref), custom_call_target="tpu_custom_call" | custom-call | tf_op jit(solution)/shard_map/final/pallas_call | solution.py:203
Async XLA Ops:
  5.5 18.8 %all-to-all-start = ((f32[32,8,128]{2,1,0:T(8,128)}), f32[32,8,128]{2,1,0:T(8,128)S(1)}, u32[]{:S(2)}, u32[]{:S(2)}) async-start(f32[32,8,128]{2,1,0:T(8,128)} %part.1), calls=%async_computation | async-start | bytes 262144 | tf_op jit(solution)/shard_map/all_to_all | solution.py:160
  24.4 0.7 copy-start

commit v4 on v3

--- a/solution.py
+++ b/solution.py
@@ -25,22 +25,26 @@
 
 
 def part_kernel(rows, seq_devs, slice_rows, lengths_ref, x_ref, o_ref, acc_ref):
-    s = pl.program_id(0)
+    p = pl.program_id(0)
+    each = x_ref.shape[1] // slice_rows
     shape = (seq_devs, rows)
     live = live_rows(rows, lengths_ref)(shape, 1)
-    mine = lax.broadcasted_iota(jnp.int32, shape, 0) == s
-    left = jnp.where(live & mine, 1.0, 0.0).astype(BF16)
-    term = jnp.dot(left, x_ref[...], preferred_element_type=F32)
-
-    @pl.when(s == 0)
-    def _():
-        acc_ref[...] = term
-
-    @pl.when(s > 0)
-    def _():
-        acc_ref[...] += term
-
-    @pl.when(s == seq_devs - 1)
+    total = jnp.zeros((seq_devs, slice_rows), F32)
+    for i in range(each):
+        mine = lax.broadcasted_iota(jnp.int32, shape, 0) == p * each + i
+        left = jnp.where(live & mine, 1.0, 0.0).astype(BF16)
+        block = x_ref[:, i * slice_rows : (i + 1) * slice_rows]
+        total = total + jnp.dot(left, block, preferred_element_type=F32)
+
+    @pl.when(p == 0)
+    def _():
+        acc_ref[...] = total
+
+    @pl.when(p > 0)
+    def _():
+        acc_ref[...] += total
+
+    @pl.when(p == pl.num_programs(0) - 1)
     def _():
         for t in range(slice_rows // LANES):
             tile = acc_ref[:, t * LANES : (t + 1) * LANES]
@@ -49,7 +53,8 @@
 
 
 def bucket_kernel(rows, slots, lengths_ref, blk_ref, off_ref, x_ref, o_ref, tag_ref, pick_ref):
-    slice_rows = x_ref.shape[1]
+    n, each = o_ref.shape[:2]
+    slice_rows = x_ref.shape[1] // each
 
     @pl.when(pl.program_id(0) == 0)
     def _():
@@ -72,9 +77,10 @@
         lane = lax.broadcasted_iota(jnp.int32, (slots, LANES), 1)
         tag_ref[...] = jnp.where(lane == HALF, tag, 0.0)
 
-    y = jnp.dot(pick_ref[...], x_ref[...], preferred_element_type=F32).astype(BF16)
-    o_ref[:, :, :slice_rows] = y.reshape(slots // CAP, CAP, slice_rows)
-    o_ref[:, :, slice_rows:] = jnp.zeros((slots // CAP, CAP, LANES), BF16)
+    for i in range(each):
+        block = x_ref[:, i * slice_rows : (i + 1) * slice_rows]
+        y = jnp.dot(pick_ref[...], block, preferred_element_type=F32).astype(BF16)
+        o_ref[:, i, :, :slice_rows] = y.reshape(n, CAP, slice_rows)
 
 
 def carry_kernel(seq_devs, slots, sums_ref, tag_ref, send_ref, o_ref):
@@ -90,7 +96,7 @@
     for s in range(seq_devs):
         both = jnp.where(odd, low[s : s + 1], high[s : s + 1])
         carry = jnp.where(lane < HALF, both, tag).astype(BF16)
-        o_ref[s * n : (s + 1) * n] = carry.reshape(n, CAP, LANES)
+        o_ref[:, s] = carry.reshape(n, CAP, LANES)
 
 
 def final_kernel(dims, ratio, smooth_ref, data_ref, carry_ref, o_ref, hot_ref, tot_ref):
@@ -115,7 +121,7 @@
         hot_ref[...] = jnp.where(off == v, 1.0, 0.0).astype(BF16)
         n = tot_ref.shape[0]
         k = lax.broadcasted_iota(jnp.int32, (n, kk), 1)
-        member = (k // (kk // seq_devs)) * x_devs + (k // (CAP * h_devs)) % x_devs
+        member = (k // CAP) % seq_devs * x_devs + k // (CAP * seq_devs * h_devs) % x_devs
         t = lax.broadcasted_iota(jnp.int32, (n, kk), 0)
         even = jnp.where(member == 2 * t, 1.0, 0.0).astype(BF16)
         odd = jnp.where(member == 2 * t + 1, 1.0, 0.0).astype(BF16)
@@ -145,11 +151,13 @@
     ratio = rows * devs / VOCAB
     params = pltpu.CompilerParams(vmem_limit_bytes=VMEM_LIMIT)
     smem = pl.BlockSpec(memory_space=pltpu.SMEM)
-    x_spec = pl.BlockSpec((rows, slice_rows), lambda s: (0, s))
+    steps = 2
+    each = seq_devs // steps
+    x_spec = pl.BlockSpec((rows, slice_rows * each), lambda s: (0, s))
 
     part = pl.pallas_call(
         functools.partial(part_kernel, rows, seq_devs, slice_rows),
-        grid=(seq_devs,),
+        grid=(steps,),
         in_specs=[smem, x_spec],
         out_specs=pl.BlockSpec((team, seq_devs, LANES), lambda s: (0, 0, 0)),
         out_shape=jax.ShapeDtypeStruct((team, seq_devs, LANES), F32),
@@ -162,14 +170,14 @@
     row_spec = pl.BlockSpec((1, rows), lambda s: (0, 0))
     send, tag = pl.pallas_call(
         functools.partial(bucket_kernel, rows, slots),
-        grid=(seq_devs,),
+        grid=(steps,),
         in_specs=[smem, row_spec, row_spec, x_spec],
         out_specs=[
-            pl.BlockSpec((vocab_devs, CAP, chunk), lambda s: (s, 0, 0)),
+            pl.BlockSpec((vocab_devs, each, CAP, chunk), lambda s: (0, s, 0, 0)),
             pl.BlockSpec((slots, LANES), lambda s: (0, 0)),
         ],
         out_shape=[
-            jax.ShapeDtypeStruct((devs, CAP, chunk), BF16),
+            jax.ShapeDtypeStruct((vocab_devs, seq_devs, CAP, chunk), BF16),
             jax.ShapeDtypeStruct((slots, LANES), F32),
         ],
         scratch_shapes=[pltpu.VMEM((slots, rows), BF16)],
@@ -189,16 +197,17 @@
             pl.BlockSpec((slots, LANES), lambda i: (0, 0)),
             pl.BlockSpec(memory_space=pl.ANY),
         ],
-        out_specs=pl.BlockSpec((devs, CAP, LANES), lambda i: (0, 0, tail)),
-        out_shape=jax.ShapeDtypeStruct((devs, CAP, chunk), BF16),
+        out_specs=pl.BlockSpec((vocab_devs, seq_devs, CAP, LANES), lambda i: (0, 0, 0, tail)),
+        out_shape=jax.ShapeDtypeStruct((vocab_devs, seq_devs, CAP, chunk), BF16),
         input_output_aliases={2: 0},
         compiler_params=params,
         name="carry",
     )(sums, tag, send)
 
-    got = lax.all_to_all(send, SEQ + VOC, split_axis=0, concat_axis=0, tiled=True)
-
-    cols = 2 * LANES
+    send = send.reshape(devs, CAP, chunk)
+    got = lax.all_to_all(send, VOC + SEQ, split_axis=0, concat_axis=0, tiled=True)
+
+    cols = slice_rows // 2
     dims = (seq_devs,) + tuple(lax.axis_size(a) for a in VOC)
     return pl.pallas_call(
         functools.partial(final_kernel, dims, ratio),

time: 164 us -> 152 us (0.927)
  the two profiles are of different devices: /device:TPU:8 before, /device:TPU:1 now
where the time goes in v4:
time: 152 us
  blocking collectives  122 us (80%)
  Pallas kernels  13.7 us (9%)
  starting transfers between devices  11.4 us (8%)
  waiting for transfers between devices  4.08 us (3%)
    all_to_all x1, blocking collectives, shards(): lax.all_to_all(send, VOC + SEQ, split_axis=0, concat_axis=0, tiled=True)  122 us
    all_to_all x1, starting transfers between devices, shards(): sums = lax.all_to_all(part, TEAM, split_axis=0, concat_axis=0, tiled=True)  11.4 us
    pallas_call x1, Pallas kernels, shards(): pl.pallas_call(functools.partial(final_kernel, dims, ratio), grid=(slice_...  4.85 us
    pallas_call x1, Pallas kernels, shards(): pl.pallas_call(functools.partial(bucket_kernel, rows, slots), grid=(steps...  4.42 us
    all_to_all x1, waiting for transfers between devices, shards(): sums = lax.all_to_all(part, TEAM, split_axis=0, concat_axis=0, tiled=True)  4.08 us
  transfers between devices with their start and end apart: 1, of which 1 were waited for; matrix products, arithmetic and copies ran while one was open for 0% of the time, Pallas kernels for 3%

profile of v4, /device:TPU:1, one launch (start us, length us, event | category | flops | bytes accessed | tf_op | source)
XLA Modules:
  0.0 151.7 jit_solution(13285340818317259154)
XLA Ops:
  0.0 2.6 %part.1 = f32[32,8,128]{2,1,0:T(8,128)} custom-call(s32[8]{0:T(128)} %lengths_ref.3, bf16[64,16384]{1,0:T(8,128)(2,1)} %x_ref.3), custom_call_target="tpu_custom_call" | custom-call | tf_op jit(solution)/shard_map/part/pallas_call | solution.py:158
  2.6 11.4 %all-to-all-start = ((f32[32,8,128]{2,1,0:T(8,128)}), f32[32,8,128]{2,1,0:T(8,128)S(1)}, u32[]{:S(2)}, u32[]{:S(2)}) async-start(f32[32,8,128]{2,1,0:T(8,128)} %part.1), calls=%async_computation | async-start | bytes 262144 | tf_op jit(solution)/shard_map/all_to_all | solution.py:168
  14.0 4.4 %bucket.1 = (bf16[64,8,2,2176]{3,2,1,0:T(2,128)(2,1)}, f32[128,128]{1,0:T(8,128)}) custom-call(s32[8]{0:T(128)} %lengths_ref.3, s32[1,64]{1,0:T(1,128)} %bitcast.6, s32[1,64]{1,0:T(1,128)} %bitcast.7, bf16[64,16384]{1,0:T(8,128)(2,1)} %x_ref.3), custom_call_target="tpu_custom_call" | custom-call | flops 268435456 | bytes 8388608 | tf_op jit(solution)/shard_map/bucket/pallas_call | solution.py:171
  18.4 4.1 %all-to-all-done.sums_ref = f32[32,8,128]{2,1,0:T(8,128)S(1)} async-done(((f32[32,8,128]{2,1,0:T(8,128)}), f32[32,8,128]{2,1,0:T(8,128)S(1)}, u32[]{:S(2)}, u32[]{:S(2)}) %all-to-all-start) | async-done | bytes 131104 | tf_op jit(solution)/shard_map/all_to_all | solution.py:168
  22.5 0.0 copy-start
  22.5 0.7 copy-done
  23.1 1.8 %carry.1 = bf16[64,8,2,2176]{3,2,1,0:T(2,128)(2,1)} custom-call(f32[32,8,128]{2,1,0:T(8,128)} %copy-done, f32[128,128]{1,0:T(8,128)} %get-tuple-element.7.tag_ref, bf16[64,8,2,2176]{3,2,1,0:T(2,128)(2,1)} %get-tuple-element.8.send_ref), custom_call_target="tpu_custom_call", output_to_operand_aliasing={{}: (2, {})} | custom-call | tf_op jit(solution)/shard_map/carry/pallas_call | solution.py:192
  25.0 121.9 %all_to_all.10.data_ref.carry_ref = bf16[512,2,2176]{2,1,0:T(2,128)(2,1)} all-to-all(bf16[512,2,2176]{2,1,0:T(2,128)(2,1)} %bitcast.4), channel_id=1, replica_groups=mesh['zlo'=4,'core'=2,'y'=8,'x'=4,'zhi'=2] {'y','x','zhi','zlo','core'}, dimensions={0} | all-to-all | bytes 8912896 | tf_op jit(solution)/shard_map/all_to_all | solution.py:208
  146.9 4.8 %final.1 = f32[2048,256]{1,0:T(8,128)} custom-call(f32[16,128]{1,0:T(8,128)} %bitcast.5, bf16[512,2,2176]{2,1,0:T(2,128)(2,1)} %all_to_all.10.data_ref.carry_ref, bf16[512,2,2176]{2,1,0:T(2,128)(2,1)} %all_to_all.10.data_ref.carry_ref), custom_call_target="tpu_custom_call" | custom-call | tf_op jit(solution)/shard_map/final/pallas_call | solution.py:212
Async XLA Ops:
  2.6 19.9 %all-to-all-start = ((f32[32,8,128]{2,1,0:T(8,128)}), f32[32,8,128]{2,1,0:T(8,128)S(1)}, u32[]{:S(2)}, u32[]{:S(2)}) async-start(f32[32,8,128]{2,1,0:T(8,128)} %part.1), calls=%async_computation | async-start | bytes 262144 | tf_op jit(solution)/shard_map/all_to_all | solution.py:168
  22.5 0.7 copy-start

commit v5 on v1

v5 whole, which is shorter than its diff:
```python
import functools

import jax
import jax.numpy as jnp
from jax import lax
from jax.experimental import pallas as pl
from jax.experimental.pallas import tpu as pltpu
from jax.sharding import Mesh, PartitionSpec as P

VOCAB = 16384
SEQ = ("zlo", "core")
VOC = ("y", "x", "zhi")
TEAM = ("y", "x")
LANES = 128
SUB = 8
CAP = 2
HALF = 64
F32 = jnp.float32
BF16 = jnp.bfloat16
MIB = 2**20


def bucket_kernel(rows, slots, lengths_ref, blk_ref, off_ref, x_ref, o_ref, pick_ref, tag_ref):
    n, each = o_ref.shape[:2]
    slice_rows = x_ref.shape[1] // each
    bound = lengths_ref[lax.axis_index(SEQ)] - lax.axis_index(VOC) * rows

    @pl.when(pl.program_id(0) == 0)
    def _():
        shape = (slots, rows)
        live = lax.broadcasted_iota(jnp.int32, shape, 1) < bound
        k = lax.broadcasted_iota(jnp.int32, shape, 0)
        hit = live & (blk_ref[...] == k // CAP)
        before = lax.broadcasted_iota(jnp.int32, (rows, rows), 0) < lax.broadcasted_iota(
            jnp.int32, (rows, rows), 1
        )
        rank = jnp.dot(
            jnp.where(hit, 1.0, 0.0).astype(BF16),
            jnp.where(before, 1.0, 0.0).astype(BF16),
            preferred_element_type=F32,
        )
        pick = hit & (rank == (k % CAP).astype(F32))
        pick_ref[...] = jnp.where(pick, 1.0, 0.0).astype(BF16)
        value = jnp.where(pick, (off_ref[...] + 1).astype(F32), 0.0)
        tag = jnp.sum(value, axis=1, keepdims=True) - 1.0
        tag_ref[...] = jnp.broadcast_to(tag, (slots, LANES))

    live = lax.broadcasted_iota(jnp.int32, (SUB, rows), 1) < bound
    left = jnp.where(live, 1.0, 0.0).astype(BF16)
    row = lax.broadcasted_iota(jnp.int32, (SUB, LANES), 0)
    lane = lax.broadcasted_iota(jnp.int32, (SUB, LANES), 1)
    for i in range(each):
        block = x_ref[:, i * slice_rows : (i + 1) * slice_rows]
        y = jnp.dot(pick_ref[...], block, preferred_element_type=F32).astype(BF16)
        o_ref[:, i, :, :slice_rows] = y.reshape(n, CAP, slice_rows)
        part = jnp.dot(left, block, preferred_element_type=F32)
        tiles = []
        for t in range(slots // SUB):
            mine = part[:, t * LANES : (t + 1) * LANES]
            mine = jnp.where(row < SUB // 2, mine, pltpu.roll(mine, HALF, 1))
            high = mine.astype(BF16).astype(F32)
            both = jnp.where(row % CAP == 0, high, mine - high)
            tag = tag_ref[t * SUB : (t + 1) * SUB, :]
            tiles.append(jnp.where(lane < HALF, both, tag))
        carry = jnp.concatenate(tiles, axis=0).astype(BF16)
        o_ref[:, i, :, slice_rows:] = carry.reshape(n, CAP, LANES)


def total_kernel(carry_ref, o_ref):
    carry = carry_ref[...].reshape(-1, LANES)
    ones = jnp.ones((SUB, carry.shape[0]), BF16)
    total = jnp.dot(ones, carry, preferred_element_type=F32)
    for m in range(o_ref.shape[0]):
        o_ref[m] = total


def count_kernel(data_ref, carry_ref, o_ref, hot_ref):
    kk = hot_ref.shape[1]
    width = hot_ref.shape[0]

    @pl.when(pl.program_id(0) == 0)
    def _():
        sel = lax.broadcasted_iota(jnp.int32, (16, LANES), 1) == HALF
        off = lax.dot_general(
            jnp.where(sel, 1.0, 0.0).astype(BF16),
            carry_ref[...].reshape(kk, LANES),
            (((1,), (1,)), ((), ())),
            preferred_element_type=F32,
        )[0:1]
        v = lax.broadcasted_iota(jnp.int32, (width, kk), 0).astype(F32)
        hot_ref[...] = jnp.where(off == v, 1.0, 0.0).astype(BF16)

    data = data_ref[...].reshape(kk, data_ref.shape[2])
    o_ref[...] = jnp.dot(hot_ref[...], data, preferred_element_type=F32)


def scale_kernel(ratio, smooth_ref, totals_ref, counts_ref, o_ref):
    tiles = counts_ref.shape[1] // LANES
    first = pl.program_id(0) * tiles
    lane = lax.broadcasted_iota(jnp.int32, (1, LANES), 1)
    for i in range(tiles):
        t = first + i
        even = totals_ref[2 * t, 0:1, :]
        odd = totals_ref[2 * t + 1, 0:1, :]
        total = jnp.where(lane < HALF, even, pltpu.roll(odd, HALF, 1))
        pseudo = smooth_ref[pl.ds(t, 1), :] * ratio
        scale = VOCAB / (total + VOCAB * pseudo)
        done = (counts_ref[:, i * LANES : (i + 1) * LANES] + pseudo) * scale
        o_ref[i * LANES : (i + 1) * LANES, :] = done.T


def shards(posteriors, token_block, token_offset, lengths, smoothing):
    rows, states = posteriors.shape
    seq_devs = lax.axis_size(SEQ)
    vocab_devs = lax.axis_size(VOC)
    devs = seq_devs * vocab_devs
    team = lax.axis_size(TEAM)
    width = VOCAB // vocab_devs
    slice_rows = states // seq_devs
    slots = vocab_devs * CAP
    chunk = slice_rows + LANES
    ratio = rows * devs / VOCAB
    steps = 2
    each = seq_devs // steps
    tail = slice_rows // LANES
    params = pltpu.CompilerParams(vmem_limit_bytes=60 * MIB)

    row_spec = pl.BlockSpec((1, rows), lambda s: (0, 0))
    send = pl.pallas_call(
        functools.partial(bucket_kernel, rows, slots),
        grid=(steps,),
        in_specs=[
            pl.BlockSpec(memory_space=pltpu.SMEM),
            row_spec,
            row_spec,
            pl.BlockSpec((rows, slice_rows * each), lambda s: (0, s)),
        ],
        out_specs=pl.BlockSpec((vocab_devs, each, CAP, chunk), lambda s: (0, s, 0, 0)),
        out_shape=jax.ShapeDtypeStruct((vocab_devs, seq_devs, CAP, chunk), BF16),
        scratch_shapes=[pltpu.VMEM((slots, rows), BF16), pltpu.VMEM((slots, LANES), F32)],
        compiler_params=pltpu.CompilerParams(vmem_limit_bytes=46 * MIB),
        name="bucket",
    )(lengths, token_block.reshape(1, rows), token_offset.reshape(1, rows), posteriors)

    send = send.reshape(devs, CAP, chunk)
    got = lax.all_to_all(send, VOC + SEQ, split_axis=0, concat_axis=0, tiled=True)

    carry_spec = pl.BlockSpec((devs, CAP, LANES), lambda p: (0, 0, tail))
    mine = pl.pallas_call(
        total_kernel,
        grid=(1,),
        in_specs=[carry_spec],
        out_specs=pl.BlockSpec((team, SUB, LANES), lambda i: (0, 0, 0)),
        out_shape=jax.ShapeDtypeStruct((team, SUB, LANES), F32),
        compiler_params=params,
        name="total",
    )(got)
    totals = lax.all_to_all(mine, TEAM, split_axis=0, concat_axis=0, tiled=True)

    cols = slice_rows // 2
    counts = pl.pallas_call(
        count_kernel,
        grid=(slice_rows // cols,),
        in_specs=[pl.BlockSpec((devs, CAP, cols), lambda p: (0, 0, p)), carry_spec],
        out_specs=pl.BlockSpec((width, cols), lambda p: (0, p)),
        out_shape=jax.ShapeDtypeStruct((width, slice_rows), F32),
        scratch_shapes=[pltpu.VMEM((width, devs * CAP), BF16)],
        compiler_params=params,
        cost_estimate=pl.CostEstimate(
            flops=2 * devs * CAP * width * slice_rows,
            bytes_accessed=2 * devs * CAP * chunk + 4 * width * slice_rows,
            transcendentals=0,
        ),
        name="count",
    )(got, got)

    return pl.pallas_call(
        functools.partial(scale_kernel, ratio),
        grid=(slice_rows // cols,),
        in_specs=[
            pl.BlockSpec((tail, LANES), lambda p: (0, 0)),
            pl.BlockSpec((team, SUB, LANES), lambda p: (0, 0, 0)),
            pl.BlockSpec((width, cols), lambda p: (0, p)),
        ],
        out_specs=pl.BlockSpec((cols, width), lambda p: (p, 0)),
        out_shape=jax.ShapeDtypeStruct((slice_rows, width), F32),
        compiler_params=params,
        name="scale",
    )(smoothing.reshape(tail, LANES), totals, counts)


def solution(mesh):
    fine = Mesh(mesh.devices.reshape(4, 2, 8, 4, 2), SEQ + VOC)
    placed = (P(SEQ + VOC, None), P(SEQ + VOC, None), P(SEQ + VOC), P(), P(SEQ))
    return jax.shard_map(
        shards, mesh=fine, in_specs=placed, out_specs=P(SEQ, VOC), check_vma=False
    )
```

time: 317 us -> 154 us (0.49); the launches traced: 312 us -> 153 us
  waiting for transfers between devices: 209 us -> 4.88 us
  blocking collectives: 27.7 us -> 127 us
  starting transfers between devices: 24.3 us -> 4.52 us
  local copies, waits for them, and re-layouts: 18.4 us -> 4.2 us
  between operations: 13.5 us -> 0.02 us
  Pallas kernels: 0 us -> 12.6 us
  matrix products: 10.5 us -> 0 us
  other arithmetic: 8.6 us -> 0 us
    psum x2 -> x0, waiting for transfers between devices: 209 us -> none  [the longest x1 136 us: shards(): joined = lax.psum(jnp.concatenate([part, place(tags, SEQ)]), SEQ)]
    all_to_all x0 -> x1, blocking collectives: none -> 127 us  [shards(): lax.all_to_all(send, VOC + SEQ, split_axis=0, concat_axis=0, tiled=True)]
    psum x2 -> x0, blocking collectives: 27.7 us -> none  [shards(): joined = lax.psum(jnp.concatenate([totals, place(tags, axis)]), axis)]
    all_to_all x1, starting transfers between devices: 24.2 us -> 4.52 us  [shards(): totals = lax.all_to_all(mine, TEAM, split_axis=0, concat_axis=0, tiled=True)]
    reshape x2 -> x0, local copies, waits for them, and re-layouts: 14.8 us -> none  [the longest x1 7.63 us: shards(): buckets.astype(jnp.bfloat16)]
    pallas_call x0 -> x4, Pallas kernels: none -> 12.6 us  [the longest x1 4.47 us: shards(): pl.pallas_call(count_kernel, grid=(slice_rows // cols,), in_specs=[pl.Blo...]
    dot_general x3 -> x0, matrix products: 10.5 us -> none  [the longest x1 5.23 us: shards(): jnp.dot(one_hot, got.reshape(-1, state_rows), preferred_element_type=jnp....]
    all_to_all x1, waiting for transfers between devices: 0.01 us -> 4.88 us  [shards(): totals = lax.all_to_all(mine, TEAM, split_axis=0, concat_axis=0, tiled=True)]
  transfers between devices with their start and end apart: 3 -> 1, of which waited for: 2 -> 1; matrix products, arithmetic and copies ran while one was open for 3% -> 0% of each run, Pallas kernels for 0% -> 3%
where the time goes in v5:
time: 154 us; the launch traced here: 153 us
  blocking collectives  127 us (82%)
  Pallas kernels  12.6 us (8%)
  waiting for transfers between devices  4.88 us (3%)
  starting transfers between devices  4.52 us (3%)
  local copies, waits for them, and re-layouts  4.2 us (3%)
    all_to_all x1, blocking collectives, shards(): lax.all_to_all(send, VOC + SEQ, split_axis=0, concat_axis=0, tiled=True)  127 us
    all_to_all x1, waiting for transfers between devices, shards(): totals = lax.all_to_all(mine, TEAM, split_axis=0, concat_axis=0, tiled=True)  4.88 us
    all_to_all x1, starting transfers between devices, shards(): totals = lax.all_to_all(mine, TEAM, split_axis=0, concat_axis=0, tiled=True)  4.52 us
    pallas_call x1, Pallas kernels, shards(): pl.pallas_call(count_kernel, grid=(slice_rows // cols,), in_specs=[pl.Blo...  4.47 us
    unnamed x10, local copies, waits for them, and re-layouts  4.2 us
    pallas_call x1, Pallas kernels, shards(): pl.pallas_call(functools.partial(bucket_kernel, rows, slots), grid=(steps...  3.25 us
  transfers between devices with their start and end apart: 1, of which 1 were waited for; matrix products, arithmetic and copies ran while one was open for 0% of the time, Pallas kernels for 3%

profile of v5, /device:TPU:1, one launch (start us, length us, event | category | flops | bytes accessed | tf_op | source)
XLA Modules:
  0.0 153.4 jit_solution(17006701574318627317)
XLA Ops:
  0.0 0.0 copy-start
  0.0 1.6 %copy-done = bf16[64,16384]{1,0:T(8,128)(2,1)S(1)} copy-done((bf16[64,16384]{1,0:T(8,128)(2,1)S(1)}, bf16[64,16384]{1,0:T(8,128)(2,1)}, u32[]{:S(2)}) %copy-start) | copy-done | bytes 2097176
  1.6 0.0 copy-start.1
  1.6 0.7 copy-done.1
  2.2 0.0 copy-start.2
  2.2 0.7 copy-done.2
  2.9 0.0 copy-start.3
  2.9 0.7 copy-done.3
  3.6 3.3 %bucket.1 = bf16[64,8,2,2176]{3,2,1,0:T(2,128)(2,1)S(1)} custom-call(s32[8]{0:T(128)S(1)} %copy-done.1, s32[1,64]{1,0:T(1,128)S(1)} %bitcast.5, s32[1,64]{1,0:T(1,128)S(1)} %bitcast.6, bf16[64,16384]{1,0:T(8,128)(2,1)S(1)} %copy-done), custom_call_target="tpu_custom_call" | custom-call | tf_op jit(solution)/shard_map/bucket/pallas_call | solution.py:129
  6.8 127.2 %all_to_all.10.carry_ref.data_ref = bf16[512,2,2176]{2,1,0:T(2,128)(2,1)} all-to-all(bf16[512,2,2176]{2,1,0:T(2,128)(2,1)S(1)} %bitcast.4), channel_id=1, replica_groups=mesh['zlo'=4,'core'=2,'y'=8,'x'=4,'zhi'=2] {'y','x','zhi','zlo','core'}, dimensions={0} | all-to-all | bytes 8912896 | tf_op jit(solution)/shard_map/all_to_all | solution.py:146
  134.0 1.8 %total.1 = f32[32,8,128]{2,1,0:T(8,128)} custom-call(bf16[512,2,2176]{2,1,0:T(2,128)(2,1)} %all_to_all.10.carry_ref.data_ref), custom_call_target="tpu_custom_call" | custom-call | tf_op jit(solution)/shard_map/total/pallas_call | solution.py:149
  135.8 4.5 %all-to-all-start.1 = ((f32[32,8,128]{2,1,0:T(8,128)}), f32[32,8,128]{2,1,0:T(8,128)S(1)}, u32[]{:S(2)}, u32[]{:S(2)}) async-start(f32[32,8,128]{2,1,0:T(8,128)} %total.1), calls=%async_computation.1 | async-start | bytes 262144 | tf_op jit(solution)/shard_map/all_to_all | solution.py:158
  140.3 4.5 %count.1.counts_ref = f32[256,2048]{1,0:T(8,128)} custom-call(bf16[512,2,2176]{2,1,0:T(2,128)(2,1)} %all_to_all.10.carry_ref.data_ref, bf16[512,2,2176]{2,1,0:T(2,128)(2,1)} %all_to_all.10.carry_ref.data_ref), custom_call_target="tpu_custom_call" | custom-call | flops 1073741824 | bytes 6553600 | tf_op jit(solution)/shard_map/count/pallas_call | solution.py:161
  144.8 4.9 %all-to-all-done.1.totals_ref = f32[32,8,128]{2,1,0:T(8,128)S(1)} async-done(((f32[32,8,128]{2,1,0:T(8,128)}), f32[32,8,128]{2,1,0:T(8,128)S(1)}, u32[]{:S(2)}, u32[]{:S(2)}) %all-to-all-start.1) | async-done | bytes 131104 | tf_op jit(solution)/shard_map/all_to_all | solution.py:158
  149.7 0.0 copy-start.4
  149.7 0.6 copy-done.4
  150.3 3.0 %scale.1 = f32[2048,256]{1,0:T(8,128)} custom-call(f32[16,128]{1,0:T(8,128)} %bitcast.7, f32[32,8,128]{2,1,0:T(8,128)} %copy-done.4, f32[256,2048]{1,0:T(8,128)} %count.1.counts_ref), custom_call_target="tpu_custom_call" | custom-call | tf_op jit(solution)/shard_map/scale/pallas_call | solution.py:177
Async XLA Ops:
  0.0 1.6 %copy-start = (bf16[64,16384]{1,0:T(8,128)(2,1)S(1)}, bf16[64,16384]{1,0:T(8,128)(2,1)}, u32[]{:S(2)}) copy-start(bf16[64,16384]{1,0:T(8,128)(2,1)} %x_ref.1) | copy-start | bytes 6291460
  1.6 0.7 copy-start.1
  2.2 0.7 copy-start.2
  2.9 0.7 copy-start.3
  135.8 13.9 %all-to-all-start.1 = ((f32[32,8,128]{2,1,0:T(8,128)}), f32[32,8,128]{2,1,0:T(8,128)S(1)}, u32[]{:S(2)}, u32[]{:S(2)}) async-start(f32[32,8,128]{2,1,0:T(8,128)} %total.1), calls=%async_computation.1 | async-start | bytes 262144 | tf_op jit(solution)/shard_map/all_to_all | solution.py:158
  149.7 0.6 copy-start.4

commit v6 on v4

--- a/solution.py
+++ b/solution.py
@@ -99,17 +99,17 @@
         o_ref[:, s] = carry.reshape(n, CAP, LANES)
 
 
-def final_kernel(dims, ratio, smooth_ref, data_ref, carry_ref, o_ref, hot_ref, tot_ref):
+def final_kernel(dims, ratio, smooth_ref, got_ref, o_ref, hot_ref, tot_ref):
     seq_devs, y_devs, x_devs, h_devs = dims
     p = pl.program_id(0)
     kk = seq_devs * y_devs * x_devs * h_devs * CAP
-    width = o_ref.shape[1]
-    cols = data_ref.shape[2]
+    cols, width = o_ref.shape
     tiles = cols // LANES
+    slice_rows = got_ref.shape[2] - LANES
 
     @pl.when(p == 0)
     def _():
-        carry = carry_ref[...].reshape(kk, LANES)
+        carry = got_ref[:, :, slice_rows:].reshape(kk, LANES)
         sel = lax.broadcasted_iota(jnp.int32, (16, LANES), 1) == HALF
         off = lax.dot_general(
             jnp.where(sel, 1.0, 0.0).astype(BF16),
@@ -130,7 +130,8 @@
         lane = lax.broadcasted_iota(jnp.int32, (n, LANES), 1)
         tot_ref[...] = jnp.where(lane < HALF, even, pltpu.roll(odd, HALF, 1))
 
-    counts = jnp.dot(hot_ref[...], data_ref[...].reshape(kk, cols), preferred_element_type=F32)
+    data = got_ref[:, :, pl.ds(pl.multiple_of(p * cols, LANES), cols)].reshape(kk, cols)
+    counts = jnp.dot(hot_ref[...], data, preferred_element_type=F32)
     for i in range(tiles):
         pseudo = smooth_ref[pl.ds(p * tiles + i, 1), :] * ratio
         scale = VOCAB / (tot_ref[pl.ds(p * tiles + i, 1), :] + VOCAB * pseudo)
@@ -200,7 +201,7 @@
         out_specs=pl.BlockSpec((vocab_devs, seq_devs, CAP, LANES), lambda i: (0, 0, 0, tail)),
         out_shape=jax.ShapeDtypeStruct((vocab_devs, seq_devs, CAP, chunk), BF16),
         input_output_aliases={2: 0},
-        compiler_params=params,
+        compiler_params=pltpu.CompilerParams(vmem_limit_bytes=60 * 2**20),
         name="carry",
     )(sums, tag, send)
 
@@ -214,8 +215,7 @@
         grid=(slice_rows // cols,),
         in_specs=[
             pl.BlockSpec((tail, LANES), lambda p: (0, 0)),
-            pl.BlockSpec((devs, CAP, cols), lambda p: (0, 0, p)),
-            pl.BlockSpec((devs, CAP, LANES), lambda p: (0, 0, tail)),
+            pl.BlockSpec(memory_space=pltpu.VMEM),
         ],
         out_specs=pl.BlockSpec((cols, width), lambda p: (p, 0)),
         out_shape=jax.ShapeDtypeStruct((slice_rows, width), F32),
@@ -223,9 +223,9 @@
             pltpu.VMEM((width, devs * CAP), BF16),
             pltpu.VMEM((tail, LANES), F32),
         ],
-        compiler_params=params,
+        compiler_params=pltpu.CompilerParams(vmem_limit_bytes=32 * 2**20),
         name="final",
-    )(smoothing.reshape(tail, LANES), got, got)
+    )(smoothing.reshape(tail, LANES), got)
 
 
 def solution(mesh):

time: 152 us -> 150 us (0.987)
  Pallas kernels: 13.7 us -> 12.1 us
    pallas_call x1, Pallas kernels: 4.85 us -> 3.2 us  [shards(): pl.pallas_call(functools.partial(final_kernel, dims, ratio), grid=(slice_...]
where the time goes in v6:
time: 150 us
  blocking collectives  122 us (81%)
  Pallas kernels  12.1 us (8%)
  starting transfers between devices  11.4 us (8%)
  waiting for transfers between devices  4.06 us (3%)
    all_to_all x1, blocking collectives, shards(): lax.all_to_all(send, VOC + SEQ, split_axis=0, concat_axis=0, tiled=True)  122 us
    all_to_all x1, starting transfers between devices, shards(): sums = lax.all_to_all(part, TEAM, split_axis=0, concat_axis=0, tiled=True)  11.4 us
    pallas_call x1, Pallas kernels, shards(): pl.pallas_call(functools.partial(bucket_kernel, rows, slots), grid=(steps...  4.44 us
    all_to_all x1, waiting for transfers between devices, shards(): sums = lax.all_to_all(part, TEAM, split_axis=0, concat_axis=0, tiled=True)  4.06 us
    pallas_call x1, Pallas kernels, shards(): pl.pallas_call(functools.partial(final_kernel, dims, ratio), grid=(slice_...  3.2 us
  transfers between devices with their start and end apart: 1, of which 1 were waited for; matrix products, arithmetic and copies ran while one was open for 0% of the time, Pallas kernels for 3%

profile of v6, /device:TPU:1, one launch (start us, length us, event | category | flops | bytes accessed | tf_op | source)
XLA Modules:
  0.0 150.0 jit_solution(17369483989496447130)
XLA Ops:
  0.0 2.6 %part.1 = f32[32,8,128]{2,1,0:T(8,128)} custom-call(s32[8]{0:T(128)} %lengths_ref.3, bf16[64,16384]{1,0:T(8,128)(2,1)} %x_ref.3), custom_call_target="tpu_custom_call" | custom-call | tf_op jit(solution)/shard_map/part/pallas_call | solution.py:159
  2.6 11.4 %all-to-all-start = ((f32[32,8,128]{2,1,0:T(8,128)}), f32[32,8,128]{2,1,0:T(8,128)S(1)}, u32[]{:S(2)}, u32[]{:S(2)}) async-start(f32[32,8,128]{2,1,0:T(8,128)} %part.1), calls=%async_computation | async-start | bytes 262144 | tf_op jit(solution)/shard_map/all_to_all | solution.py:169
  14.0 4.4 %bucket.1 = (bf16[64,8,2,2176]{3,2,1,0:T(2,128)(2,1)}, f32[128,128]{1,0:T(8,128)}) custom-call(s32[8]{0:T(128)} %lengths_ref.3, s32[1,64]{1,0:T(1,128)} %bitcast.6, s32[1,64]{1,0:T(1,128)} %bitcast.7, bf16[64,16384]{1,0:T(8,128)(2,1)} %x_ref.3), custom_call_target="tpu_custom_call" | custom-call | flops 268435456 | bytes 8388608 | tf_op jit(solution)/shard_map/bucket/pallas_call | solution.py:172
  18.4 4.1 %all-to-all-done.sums_ref = f32[32,8,128]{2,1,0:T(8,128)S(1)} async-done(((f32[32,8,128]{2,1,0:T(8,128)}), f32[32,8,128]{2,1,0:T(8,128)S(1)}, u32[]{:S(2)}, u32[]{:S(2)}) %all-to-all-start) | async-done | bytes 131104 | tf_op jit(solution)/shard_map/all_to_all | solution.py:169
  22.5 0.0 copy-start.1
  22.5 0.7 copy-done.1
  23.1 1.9 %carry.1 = bf16[64,8,2,2176]{3,2,1,0:T(2,128)(2,1)} custom-call(f32[32,8,128]{2,1,0:T(8,128)} %copy-done.1, f32[128,128]{1,0:T(8,128)} %get-tuple-element.7.tag_ref, bf16[64,8,2,2176]{3,2,1,0:T(2,128)(2,1)} %get-tuple-element.8.send_ref), custom_call_target="tpu_custom_call", output_to_operand_aliasing={{}: (2, {})} | custom-call | tf_op jit(solution)/shard_map/carry/pallas_call | solution.py:193
  25.0 0.0 copy-start
  25.0 121.8 %all_to_all.10.got_ref = bf16[512,2,2176]{2,1,0:T(2,128)(2,1)S(1)} all-to-all(bf16[512,2,2176]{2,1,0:T(2,128)(2,1)} %bitcast.5), channel_id=1, replica_groups=mesh['zlo'=4,'core'=2,'y'=8,'x'=4,'zhi'=2] {'y','x','zhi','zlo','core'}, dimensions={0} | all-to-all | bytes 8912896 | tf_op jit(solution)/shard_map/all_to_all | solution.py:209
  146.8 0.0 copy-done
  146.8 3.2 %final.1 = f32[2048,256]{1,0:T(8,128)} custom-call(f32[16,128]{1,0:T(8,128)S(1)} %bitcast.4, bf16[512,2,2176]{2,1,0:T(2,128)(2,1)S(1)} %all_to_all.10.got_ref), custom_call_target="tpu_custom_call" | custom-call | tf_op jit(solution)/shard_map/final/pallas_call | solution.py:213
Async XLA Ops:
  2.6 19.9 %all-to-all-start = ((f32[32,8,128]{2,1,0:T(8,128)}), f32[32,8,128]{2,1,0:T(8,128)S(1)}, u32[]{:S(2)}, u32[]{:S(2)}) async-start(f32[32,8,128]{2,1,0:T(8,128)} %part.1), calls=%async_computation | async-start | bytes 262144 | tf_op jit(solution)/shard_map/all_to_all | solution.py:169
  22.5 0.7 copy-start.1
  25.0 121.8 %copy-start = (f32[2048]{0:T(1024)S(1)}, f32[2048]{0:T(1024)}, u32[]{:S(2)}) copy-start(f32[2048]{0:T(1024)} %param.9) | copy-start | bytes 24580

commit v7 on v6

--- a/solution.py
+++ b/solution.py
@@ -8,9 +8,9 @@
 from jax.sharding import Mesh, PartitionSpec as P
 
 VOCAB = 16384
-SEQ = ("zlo", "core")
-VOC = ("y", "x", "zhi")
-TEAM = ("zlo", "core", "x")
+SEQ = ("z1", "z0", "core")
+VOC = ("yh", "yl", "x", "zhi")
+TEAM = ("z0", "core", "yl", "x")
 LANES = 128
 CAP = 2
 HALF = 64
@@ -46,10 +46,13 @@
 
     @pl.when(p == pl.num_programs(0) - 1)
     def _():
+        n = seq_devs // 2
+        lane = lax.broadcasted_iota(jnp.int32, (n, LANES), 1)
         for t in range(slice_rows // LANES):
             tile = acc_ref[:, t * LANES : (t + 1) * LANES]
-            o_ref[2 * t] = tile
-            o_ref[2 * t + 1] = pltpu.roll(tile, HALF, 1)
+            turned = pltpu.roll(tile, HALF, 1)
+            o_ref[2 * t] = jnp.where(lane < HALF, tile[:n], turned[n:])
+            o_ref[2 * t + 1] = jnp.where(lane < HALF, turned[:n], tile[n:])
 
 
 def bucket_kernel(rows, slots, lengths_ref, blk_ref, off_ref, x_ref, o_ref, tag_ref, pick_ref):
@@ -86,6 +89,7 @@
 def carry_kernel(seq_devs, slots, sums_ref, tag_ref, send_ref, o_ref):
     del send_ref
     total = jnp.sum(sums_ref[...], axis=0)
+    total = jnp.concatenate([total, pltpu.roll(total, HALF, 1)], axis=0)
     high = total.astype(BF16).astype(F32)
     low = total - high
     shape = (slots, LANES)
@@ -99,10 +103,10 @@
         o_ref[:, s] = carry.reshape(n, CAP, LANES)
 
 
-def final_kernel(dims, ratio, smooth_ref, got_ref, o_ref, hot_ref, tot_ref):
-    seq_devs, y_devs, x_devs, h_devs = dims
+def final_kernel(seq_devs, team_axes, ratio, smooth_ref, got_ref, o_ref, hot_ref, tot_ref):
+    team_seq, team_voc, h_devs = team_axes
     p = pl.program_id(0)
-    kk = seq_devs * y_devs * x_devs * h_devs * CAP
+    kk = got_ref.shape[0] * CAP
     cols, width = o_ref.shape
     tiles = cols // LANES
     slice_rows = got_ref.shape[2] - LANES
@@ -121,7 +125,7 @@
         hot_ref[...] = jnp.where(off == v, 1.0, 0.0).astype(BF16)
         n = tot_ref.shape[0]
         k = lax.broadcasted_iota(jnp.int32, (n, kk), 1)
-        member = (k // CAP) % seq_devs * x_devs + k // (CAP * seq_devs * h_devs) % x_devs
+        member = k // CAP % team_seq * team_voc + k // (CAP * seq_devs * h_devs) % team_voc
         t = lax.broadcasted_iota(jnp.int32, (n, kk), 0)
         even = jnp.where(member == 2 * t, 1.0, 0.0).astype(BF16)
         odd = jnp.where(member == 2 * t + 1, 1.0, 0.0).astype(BF16)
@@ -160,8 +164,8 @@
         functools.partial(part_kernel, rows, seq_devs, slice_rows),
         grid=(steps,),
         in_specs=[smem, x_spec],
-        out_specs=pl.BlockSpec((team, seq_devs, LANES), lambda s: (0, 0, 0)),
-        out_shape=jax.ShapeDtypeStruct((team, seq_devs, LANES), F32),
+        out_specs=pl.BlockSpec((team, seq_devs // 2, LANES), lambda s: (0, 0, 0)),
+        out_shape=jax.ShapeDtypeStruct((team, seq_devs // 2, LANES), F32),
         scratch_shapes=[pltpu.VMEM((seq_devs, slice_rows), F32)],
         compiler_params=params,
         name="part",
@@ -194,7 +198,7 @@
         functools.partial(carry_kernel, seq_devs, slots),
         grid=(1,),
         in_specs=[
-            pl.BlockSpec((team, seq_devs, LANES), lambda i: (0, 0, 0)),
+            pl.BlockSpec((team, seq_devs // 2, LANES), lambda i: (0, 0, 0)),
             pl.BlockSpec((slots, LANES), lambda i: (0, 0)),
             pl.BlockSpec(memory_space=pl.ANY),
         ],
@@ -209,9 +213,9 @@
     got = lax.all_to_all(send, VOC + SEQ, split_axis=0, concat_axis=0, tiled=True)
 
     cols = slice_rows // 2
-    dims = (seq_devs,) + tuple(lax.axis_size(a) for a in VOC)
+    team_axes = (lax.axis_size(TEAM[:2]), lax.axis_size(TEAM[2:]), lax.axis_size(VOC[-1]))
     return pl.pallas_call(
-        functools.partial(final_kernel, dims, ratio),
+        functools.partial(final_kernel, seq_devs, team_axes, ratio),
         grid=(slice_rows // cols,),
         in_specs=[
             pl.BlockSpec((tail, LANES), lambda p: (0, 0)),
@@ -229,7 +233,7 @@
 
 
 def solution(mesh):
-    fine = Mesh(mesh.devices.reshape(4, 2, 8, 4, 2), SEQ + VOC)
+    fine = Mesh(mesh.devices.reshape(2, 2, 2, 4, 2, 4, 2), SEQ + VOC)
     placed = (P(SEQ + VOC, None), P(SEQ + VOC, None), P(SEQ + VOC), P(), P(SEQ))
     return jax.shard_map(
         shards, mesh=fine, in_specs=placed, out_specs=P(SEQ, VOC), check_vma=False

time: 150 us -> 147 us (0.980)
  waiting for transfers between devices: 4.06 us -> 2.43 us
    all_to_all x1, waiting for transfers between devices: 4.06 us -> 2.43 us  [shards(): sums = lax.all_to_all(part, TEAM, split_axis=0, concat_axis=0, tiled=True)]
where the time goes in v7:
time: 147 us; the launch traced here: 146 us
  blocking collectives  121 us (82%)
  Pallas kernels  12.1 us (8%)
  starting transfers between devices  10.4 us (7%)
  waiting for transfers between devices  2.43 us (2%)
    all_to_all x1, blocking collectives, shards(): lax.all_to_all(send, VOC + SEQ, split_axis=0, concat_axis=0, tiled=True)  121 us
    all_to_all x1, starting transfers between devices, shards(): sums = lax.all_to_all(part, TEAM, split_axis=0, concat_axis=0, tiled=True)  10.4 us
    pallas_call x1, Pallas kernels, shards(): pl.pallas_call(functools.partial(bucket_kernel, rows, slots), grid=(steps...  4.45 us
    pallas_call x1, Pallas kernels, shards(): pl.pallas_call(functools.partial(final_kernel, seq_devs, team_axes, ratio...  3.2 us
  transfers between devices with their start and end apart: 1, of which 1 were waited for; matrix products, arithmetic and copies ran while one was open for 0% of the time, Pallas kernels for 3%

profile of v7, /device:TPU:1, one launch (start us, length us, event | category | flops | bytes accessed | tf_op | source)
XLA Modules:
  0.0 146.3 jit_solution(7001296943010324464)
XLA Ops:
  0.0 2.5 %part.1 = f32[32,4,128]{2,1,0:T(4,128)} custom-call(s32[8]{0:T(128)} %lengths_ref.3, bf16[64,16384]{1,0:T(8,128)(2,1)} %x_ref.3), custom_call_target="tpu_custom_call" | custom-call | tf_op jit(solution)/shard_map/part/pallas_call | solution.py:163
  2.5 10.4 %all-to-all-start = ((f32[32,4,128]{2,1,0:T(4,128)}), f32[32,4,128]{2,1,0:T(4,128)S(1)}, u32[]{:S(2)}, u32[]{:S(2)}) async-start(f32[32,4,128]{2,1,0:T(4,128)} %part.1), calls=%async_computation | async-start | bytes 131072 | tf_op jit(solution)/shard_map/all_to_all | solution.py:173
  13.0 4.5 %bucket.1 = (bf16[64,8,2,2176]{3,2,1,0:T(2,128)(2,1)}, f32[128,128]{1,0:T(8,128)}) custom-call(s32[8]{0:T(128)} %lengths_ref.3, s32[1,64]{1,0:T(1,128)} %bitcast.6, s32[1,64]{1,0:T(1,128)} %bitcast.7, bf16[64,16384]{1,0:T(8,128)(2,1)} %x_ref.3), custom_call_target="tpu_custom_call" | custom-call | flops 268435456 | bytes 8388608 | tf_op jit(solution)/shard_map/bucket/pallas_call | solution.py:176
  17.4 2.4 %all-to-all-done.sums_ref = f32[32,4,128]{2,1,0:T(4,128)S(1)} async-done(((f32[32,4,128]{2,1,0:T(4,128)}), f32[32,4,128]{2,1,0:T(4,128)S(1)}, u32[]{:S(2)}, u32[]{:S(2)}) %all-to-all-start) | async-done | bytes 65568 | tf_op jit(solution)/shard_map/all_to_all | solution.py:173
  19.9 0.0 copy-start.1
  19.9 0.6 copy-done.1
  20.5 1.9 %carry.1 = bf16[64,8,2,2176]{3,2,1,0:T(2,128)(2,1)} custom-call(f32[32,4,128]{2,1,0:T(4,128)} %copy-done.1, f32[128,128]{1,0:T(8,128)} %get-tuple-element.7.tag_ref, bf16[64,8,2,2176]{3,2,1,0:T(2,128)(2,1)} %get-tuple-element.8.send_ref), custom_call_target="tpu_custom_call", output_to_operand_aliasing={{}: (2, {})} | custom-call | tf_op jit(solution)/shard_map/carry/pallas_call | solution.py:197
  22.4 0.0 copy-start
  22.4 120.6 %all_to_all.10.got_ref = bf16[512,2,2176]{2,1,0:T(2,128)(2,1)S(1)} all-to-all(bf16[512,2,2176]{2,1,0:T(2,128)(2,1)} %bitcast.5), channel_id=1, replica_groups=mesh['z1'=2,'z0'=2,'core'=2,'yh'=4,'yl'=2,'x'=4,'zhi'=2] {'yh','yl','x',..., dimensions={0} | all-to-all | bytes 8912896 | tf_op jit(solution)/shard_map/all_to_all | solution.py:213
  143.1 0.0 copy-done
  143.1 3.2 %final.1 = f32[2048,256]{1,0:T(8,128)} custom-call(f32[16,128]{1,0:T(8,128)S(1)} %bitcast.4, bf16[512,2,2176]{2,1,0:T(2,128)(2,1)S(1)} %all_to_all.10.got_ref), custom_call_target="tpu_custom_call" | custom-call | tf_op jit(solution)/shard_map/final/pallas_call | solution.py:217
Async XLA Ops:
  2.5 17.3 %all-to-all-start = ((f32[32,4,128]{2,1,0:T(4,128)}), f32[32,4,128]{2,1,0:T(4,128)S(1)}, u32[]{:S(2)}, u32[]{:S(2)}) async-start(f32[32,4,128]{2,1,0:T(4,128)} %part.1), calls=%async_computation | async-start | bytes 131072 | tf_op jit(solution)/shard_map/all_to_all | solution.py:173
  19.9 0.6 copy-start.1
  22.4 120.6 %copy-start = (f32[2048]{0:T(1024)S(1)}, f32[2048]{0:T(1024)}, u32[]{:S(2)}) copy-start(f32[2048]{0:T(1024)} %param.9) | copy-start | bytes 24580

commit v8 on v7

--- a/solution.py
+++ b/solution.py
@@ -55,7 +55,7 @@
             o_ref[2 * t + 1] = jnp.where(lane < HALF, turned[:n], tile[n:])
 
 
-def bucket_kernel(rows, slots, lengths_ref, blk_ref, off_ref, x_ref, o_ref, tag_ref, pick_ref):
+def bucket_kernel(rows, slots, lengths_ref, blk_ref, off_ref, x_ref, o_ref, pick_ref):
     n, each = o_ref.shape[:2]
     slice_rows = x_ref.shape[1] // each
 
@@ -78,7 +78,8 @@
         value = jnp.where(pick, (off_ref[...] + 1).astype(F32), 0.0)
         tag = jnp.sum(value, axis=1, keepdims=True) - 1.0
         lane = lax.broadcasted_iota(jnp.int32, (slots, LANES), 1)
-        tag_ref[...] = jnp.where(lane == HALF, tag, 0.0)
+        tag = jnp.where(lane == HALF, tag, 0.0).astype(BF16)
+        o_ref[:, 0, :, slice_rows:] = tag.reshape(n, CAP, LANES)
 
     for i in range(each):
         block = x_ref[:, i * slice_rows : (i + 1) * slice_rows]
@@ -86,8 +87,7 @@
         o_ref[:, i, :, :slice_rows] = y.reshape(n, CAP, slice_rows)
 
 
-def carry_kernel(seq_devs, slots, sums_ref, tag_ref, send_ref, o_ref):
-    del send_ref
+def carry_kernel(seq_devs, slots, sums_ref, tag_ref, o_ref):
     total = jnp.sum(sums_ref[...], axis=0)
     total = jnp.concatenate([total, pltpu.roll(total, HALF, 1)], axis=0)
     high = total.astype(BF16).astype(F32)
@@ -95,7 +95,7 @@
     shape = (slots, LANES)
     odd = lax.broadcasted_iota(jnp.int32, shape, 0) % CAP == 1
     lane = lax.broadcasted_iota(jnp.int32, shape, 1)
-    tag = tag_ref[...]
+    tag = tag_ref[...].reshape(slots, LANES).astype(F32)
     n = slots // CAP
     for s in range(seq_devs):
         both = jnp.where(odd, low[s : s + 1], high[s : s + 1])
@@ -173,18 +173,12 @@
     sums = lax.all_to_all(part, TEAM, split_axis=0, concat_axis=0, tiled=True)
 
     row_spec = pl.BlockSpec((1, rows), lambda s: (0, 0))
-    send, tag = pl.pallas_call(
+    send = pl.pallas_call(
         functools.partial(bucket_kernel, rows, slots),
         grid=(steps,),
         in_specs=[smem, row_spec, row_spec, x_spec],
-        out_specs=[
-            pl.BlockSpec((vocab_devs, each, CAP, chunk), lambda s: (0, s, 0, 0)),
-            pl.BlockSpec((slots, LANES), lambda s: (0, 0)),
-        ],
-        out_shape=[
-            jax.ShapeDtypeStruct((vocab_devs, seq_devs, CAP, chunk), BF16),
-            jax.ShapeDtypeStruct((slots, LANES), F32),
-        ],
+        out_specs=pl.BlockSpec((vocab_devs, each, CAP, chunk), lambda s: (0, s, 0, 0)),
+        out_shape=jax.ShapeDtypeStruct((vocab_devs, seq_devs, CAP, chunk), BF16),
         scratch_shapes=[pltpu.VMEM((slots, rows), BF16)],
         compiler_params=params,
         cost_estimate=pl.CostEstimate(
@@ -198,16 +192,15 @@
         functools.partial(carry_kernel, seq_devs, slots),
         grid=(1,),
         in_specs=[
-            pl.BlockSpec((team, seq_devs // 2, LANES), lambda i: (0, 0, 0)),
-            pl.BlockSpec((slots, LANES), lambda i: (0, 0)),
-            pl.BlockSpec(memory_space=pl.ANY),
+            pl.BlockSpec(memory_space=pltpu.VMEM),
+            pl.BlockSpec((vocab_devs, 1, CAP, LANES), lambda i: (0, 0, 0, tail)),
         ],
         out_specs=pl.BlockSpec((vocab_devs, seq_devs, CAP, LANES), lambda i: (0, 0, 0, tail)),
         out_shape=jax.ShapeDtypeStruct((vocab_devs, seq_devs, CAP, chunk), BF16),
-        input_output_aliases={2: 0},
-        compiler_params=pltpu.CompilerParams(vmem_limit_bytes=60 * 2**20),
+        input_output_aliases={1: 0},
+        compiler_params=pltpu.CompilerParams(vmem_limit_bytes=52 * 2**20),
         name="carry",
-    )(sums, tag, send)
+    )(sums, send)
 
     send = send.reshape(devs, CAP, chunk)
     got = lax.all_to_all(send, VOC + SEQ, split_axis=0, concat_axis=0, tiled=True)

time: 147 us -> 146 us (level)
  no operation moved by 1% of the time
where the time goes in v8:
time: 146 us; the launch traced here: 145 us
  blocking collectives  121 us (83%)
  Pallas kernels  11.9 us (8%)
  starting transfers between devices  10.4 us (7%)
  waiting for transfers between devices  2.49 us (2%)
    all_to_all x1, blocking collectives, shards(): lax.all_to_all(send, VOC + SEQ, split_axis=0, concat_axis=0, tiled=True)  121 us
    all_to_all x1, starting transfers between devices, shards(): sums = lax.all_to_all(part, TEAM, split_axis=0, concat_axis=0, tiled=True)  10.4 us
    pallas_call x1, Pallas kernels, shards(): pl.pallas_call(functools.partial(bucket_kernel, rows, slots), grid=(steps...  4.39 us
    pallas_call x1, Pallas kernels, shards(): pl.pallas_call(functools.partial(final_kernel, seq_devs, team_axes, ratio...  3.2 us
  transfers between devices with their start and end apart: 1, of which 1 were waited for; matrix products, arithmetic and copies ran while one was open for 0% of the time, Pallas kernels for 3%

profile of v8, /device:TPU:1, one launch (start us, length us, event | category | flops | bytes accessed | tf_op | source)
XLA Modules:
  0.0 145.5 jit_solution(2148059121145104919)
XLA Ops:
  0.0 2.5 %part.1 = f32[32,4,128]{2,1,0:T(4,128)} custom-call(s32[8]{0:T(128)} %lengths_ref.3, bf16[64,16384]{1,0:T(8,128)(2,1)} %x_ref.3), custom_call_target="tpu_custom_call" | custom-call | tf_op jit(solution)/shard_map/part/pallas_call | solution.py:163
  2.5 10.4 %all-to-all-start = ((f32[32,4,128]{2,1,0:T(4,128)}), f32[32,4,128]{2,1,0:T(4,128)S(1)}, u32[]{:S(2)}, u32[]{:S(2)}) async-start(f32[32,4,128]{2,1,0:T(4,128)} %part.1), calls=%async_computation | async-start | bytes 131072 | tf_op jit(solution)/shard_map/all_to_all | solution.py:173
  13.0 4.4 %bucket.1.tag_ref = bf16[64,8,2,2176]{3,2,1,0:T(2,128)(2,1)} custom-call(s32[8]{0:T(128)} %lengths_ref.3, s32[1,64]{1,0:T(1,128)} %bitcast.6, s32[1,64]{1,0:T(1,128)} %bitcast.7, bf16[64,16384]{1,0:T(8,128)(2,1)} %x_ref.3), custom_call_target="tpu_custom_call" | custom-call | flops 268435456 | bytes 8388608 | tf_op jit(solution)/shard_map/bucket/pallas_call | solution.py:176
  17.4 2.5 %all-to-all-done.sums_ref = f32[32,4,128]{2,1,0:T(4,128)S(1)} async-done(((f32[32,4,128]{2,1,0:T(4,128)}), f32[32,4,128]{2,1,0:T(4,128)S(1)}, u32[]{:S(2)}, u32[]{:S(2)}) %all-to-all-start) | async-done | bytes 65568 | tf_op jit(solution)/shard_map/all_to_all | solution.py:173
  19.9 1.8 %carry.1 = bf16[64,8,2,2176]{3,2,1,0:T(2,128)(2,1)} custom-call(f32[32,4,128]{2,1,0:T(4,128)S(1)} %all-to-all-done.sums_ref, bf16[64,8,2,2176]{3,2,1,0:T(2,128)(2,1)} %bucket.1.tag_ref), custom_call_target="tpu_custom_call", output_to_operand_aliasing={{}: (1, {})} | custom-call | tf_op jit(solution)/shard_map/carry/pallas_call | solution.py:191
  21.7 0.0 copy-start
  21.7 120.6 %all_to_all.10.got_ref = bf16[512,2,2176]{2,1,0:T(2,128)(2,1)S(1)} all-to-all(bf16[512,2,2176]{2,1,0:T(2,128)(2,1)} %bitcast.5), channel_id=1, replica_groups=mesh['z1'=2,'z0'=2,'core'=2,'yh'=4,'yl'=2,'x'=4,'zhi'=2] {'yh','yl','x',..., dimensions={0} | all-to-all | bytes 8912896 | tf_op jit(solution)/shard_map/all_to_all | solution.py:206
  142.3 0.0 copy-done
  142.3 3.2 %final.1 = f32[2048,256]{1,0:T(8,128)} custom-call(f32[16,128]{1,0:T(8,128)S(1)} %bitcast.4, bf16[512,2,2176]{2,1,0:T(2,128)(2,1)S(1)} %all_to_all.10.got_ref), custom_call_target="tpu_custom_call" | custom-call | tf_op jit(solution)/shard_map/final/pallas_call | solution.py:210
Async XLA Ops:
  2.5 17.3 %all-to-all-start = ((f32[32,4,128]{2,1,0:T(4,128)}), f32[32,4,128]{2,1,0:T(4,128)S(1)}, u32[]{:S(2)}, u32[]{:S(2)}) async-start(f32[32,4,128]{2,1,0:T(4,128)} %part.1), calls=%async_computation | async-start | bytes 131072 | tf_op jit(solution)/shard_map/all_to_all | solution.py:173
  21.7 120.6 %copy-start = (f32[2048]{0:T(1024)S(1)}, f32[2048]{0:T(1024)}, u32[]{:S(2)}) copy-start(f32[2048]{0:T(1024)} %param.9) | copy-start | bytes 24580

commit v9 on v8

--- a/solution.py
+++ b/solution.py
@@ -108,7 +108,6 @@
     p = pl.program_id(0)
     kk = got_ref.shape[0] * CAP
     cols, width = o_ref.shape
-    tiles = cols // LANES
     slice_rows = got_ref.shape[2] - LANES
 
     @pl.when(p == 0)
@@ -134,13 +133,16 @@
         lane = lax.broadcasted_iota(jnp.int32, (n, LANES), 1)
         tot_ref[...] = jnp.where(lane < HALF, even, pltpu.roll(odd, HALF, 1))
 
-    data = got_ref[:, :, pl.ds(pl.multiple_of(p * cols, LANES), cols)].reshape(kk, cols)
-    counts = jnp.dot(hot_ref[...], data, preferred_element_type=F32)
-    for i in range(tiles):
-        pseudo = smooth_ref[pl.ds(p * tiles + i, 1), :] * ratio
-        scale = VOCAB / (tot_ref[pl.ds(p * tiles + i, 1), :] + VOCAB * pseudo)
-        done = (counts[:, i * LANES : (i + 1) * LANES] + pseudo) * scale
-        o_ref[i * LANES : (i + 1) * LANES, :] = done.T
+    half = cols // 2
+    for q in range(2):
+        data = got_ref[:, :, q * half : (q + 1) * half].reshape(kk, half)
+        counts = jnp.dot(hot_ref[...], data, preferred_element_type=F32)
+        for i in range(half // LANES):
+            t = q * (half // LANES) + i
+            pseudo = smooth_ref[t : t + 1, :] * ratio
+            scale = VOCAB / (tot_ref[t : t + 1, :] + VOCAB * pseudo)
+            done = (counts[:, i * LANES : (i + 1) * LANES] + pseudo) * scale
+            o_ref[t * LANES : (t + 1) * LANES, :] = done.T
 
 
 def shards(posteriors, token_block, token_offset, lengths, smoothing):
@@ -205,7 +207,7 @@
     send = send.reshape(devs, CAP, chunk)
     got = lax.all_to_all(send, VOC + SEQ, split_axis=0, concat_axis=0, tiled=True)
 
-    cols = slice_rows // 2
+    cols = slice_rows
     team_axes = (lax.axis_size(TEAM[:2]), lax.axis_size(TEAM[2:]), lax.axis_size(VOC[-1]))
     return pl.pallas_call(
         functools.partial(final_kernel, seq_devs, team_axes, ratio),

time: 146 us -> 146 us (level)
  no operation moved by 1% of the time
where the time goes in v9:
time: 146 us; the launch traced here: 145 us
  blocking collectives  121 us (83%)
  Pallas kernels  11.7 us (8%)
  starting transfers between devices  10.4 us (7%)
  waiting for transfers between devices  2.49 us (2%)
    all_to_all x1, blocking collectives, shards(): lax.all_to_all(send, VOC + SEQ, split_axis=0, concat_axis=0, tiled=True)  121 us
    all_to_all x1, starting transfers between devices, shards(): sums = lax.all_to_all(part, TEAM, split_axis=0, concat_axis=0, tiled=True)  10.4 us
    pallas_call x1, Pallas kernels, shards(): pl.pallas_call(functools.partial(bucket_kernel, rows, slots), grid=(steps...  4.39 us
    pallas_call x1, Pallas kernels, shards(): pl.pallas_call(functools.partial(final_kernel, seq_devs, team_axes, ratio...  2.98 us
  transfers between devices with their start and end apart: 1, of which 1 were waited for; matrix products, arithmetic and copies ran while one was open for 0% of the time, Pallas kernels for 3%

profile of v9, /device:TPU:1, one launch (start us, length us, event | category | flops | bytes accessed | tf_op | source)
XLA Modules:
  0.0 145.3 jit_solution(10125920458151733260)
XLA Ops:
  0.0 2.5 %part.1 = f32[32,4,128]{2,1,0:T(4,128)} custom-call(s32[8]{0:T(128)} %lengths_ref.3, bf16[64,16384]{1,0:T(8,128)(2,1)} %x_ref.3), custom_call_target="tpu_custom_call" | custom-call | tf_op jit(solution)/shard_map/part/pallas_call | solution.py:165
  2.5 10.4 %all-to-all-start = ((f32[32,4,128]{2,1,0:T(4,128)}), f32[32,4,128]{2,1,0:T(4,128)S(1)}, u32[]{:S(2)}, u32[]{:S(2)}) async-start(f32[32,4,128]{2,1,0:T(4,128)} %part.1), calls=%async_computation | async-start | bytes 131072 | tf_op jit(solution)/shard_map/all_to_all | solution.py:175
  13.0 4.4 %bucket.1.tag_ref = bf16[64,8,2,2176]{3,2,1,0:T(2,128)(2,1)} custom-call(s32[8]{0:T(128)} %lengths_ref.3, s32[1,64]{1,0:T(1,128)} %bitcast.6, s32[1,64]{1,0:T(1,128)} %bitcast.7, bf16[64,16384]{1,0:T(8,128)(2,1)} %x_ref.3), custom_call_target="tpu_custom_call" | custom-call | flops 268435456 | bytes 8388608 | tf_op jit(solution)/shard_map/bucket/pallas_call | solution.py:178
  17.4 2.5 %all-to-all-done.sums_ref = f32[32,4,128]{2,1,0:T(4,128)S(1)} async-done(((f32[32,4,128]{2,1,0:T(4,128)}), f32[32,4,128]{2,1,0:T(4,128)S(1)}, u32[]{:S(2)}, u32[]{:S(2)}) %all-to-all-start) | async-done | bytes 65568 | tf_op jit(solution)/shard_map/all_to_all | solution.py:175
  19.9 1.8 %carry.1 = bf16[64,8,2,2176]{3,2,1,0:T(2,128)(2,1)} custom-call(f32[32,4,128]{2,1,0:T(4,128)S(1)} %all-to-all-done.sums_ref, bf16[64,8,2,2176]{3,2,1,0:T(2,128)(2,1)} %bucket.1.tag_ref), custom_call_target="tpu_custom_call", output_to_operand_aliasing={{}: (1, {})} | custom-call | tf_op jit(solution)/shard_map/carry/pallas_call | solution.py:193
  21.7 0.0 copy-start
  21.7 120.6 %all_to_all.10.got_ref = bf16[512,2,2176]{2,1,0:T(2,128)(2,1)S(1)} all-to-all(bf16[512,2,2176]{2,1,0:T(2,128)(2,1)} %bitcast.5), channel_id=1, replica_groups=mesh['z1'=2,'z0'=2,'core'=2,'yh'=4,'yl'=2,'x'=4,'zhi'=2] {'yh','yl','x',..., dimensions={0} | all-to-all | bytes 8912896 | tf_op jit(solution)/shard_map/all_to_all | solution.py:208
  142.3 0.0 copy-done
  142.3 3.0 %final.1 = f32[2048,256]{1,0:T(8,128)} custom-call(f32[16,128]{1,0:T(8,128)S(1)} %bitcast.4, bf16[512,2,2176]{2,1,0:T(2,128)(2,1)S(1)} %all_to_all.10.got_ref), custom_call_target="tpu_custom_call" | custom-call | tf_op jit(solution)/shard_map/final/pallas_call | solution.py:212
Async XLA Ops:
  2.5 17.3 %all-to-all-start = ((f32[32,4,128]{2,1,0:T(4,128)}), f32[32,4,128]{2,1,0:T(4,128)S(1)}, u32[]{:S(2)}, u32[]{:S(2)}) async-start(f32[32,4,128]{2,1,0:T(4,128)} %part.1), calls=%async_computation | async-start | bytes 131072 | tf_op jit(solution)/shard_map/all_to_all | solution.py:175
  21.7 120.6 %copy-start = (f32[2048]{0:T(1024)S(1)}, f32[2048]{0:T(1024)}, u32[]{:S(2)}) copy-start(f32[2048]{0:T(1024)} %param.9) | copy-start | bytes 24580

commit v10 on v8

--- a/solution.py
+++ b/solution.py
@@ -10,7 +10,7 @@
 VOCAB = 16384
 SEQ = ("z1", "z0", "core")
 VOC = ("yh", "yl", "x", "zhi")
-TEAM = ("z0", "core", "yl", "x")
+TEAM = ("core", "z0", "yl", "x")
 LANES = 128
 CAP = 2
 HALF = 64
@@ -125,7 +125,8 @@
         hot_ref[...] = jnp.where(off == v, 1.0, 0.0).astype(BF16)
         n = tot_ref.shape[0]
         k = lax.broadcasted_iota(jnp.int32, (n, kk), 1)
-        member = k // CAP % team_seq * team_voc + k // (CAP * seq_devs * h_devs) % team_voc
+        pair = k // CAP % 2 * (team_seq // 2) + k // (CAP * 2) % (team_seq // 2)
+        member = pair * team_voc + k // (CAP * seq_devs * h_devs) % team_voc
         t = lax.broadcasted_iota(jnp.int32, (n, kk), 0)
         even = jnp.where(member == 2 * t, 1.0, 0.0).astype(BF16)
         odd = jnp.where(member == 2 * t + 1, 1.0, 0.0).astype(BF16)

time: 146 us -> 146 us (level)
  no operation moved by 1% of the time
where the time goes in v10:
time: 146 us
  blocking collectives  121 us (83%)
  Pallas kernels  11.9 us (8%)
  starting transfers between devices  10.5 us (7%)
  waiting for transfers between devices  2.03 us (1%)
    all_to_all x1, blocking collectives, shards(): lax.all_to_all(send, VOC + SEQ, split_axis=0, concat_axis=0, tiled=True)  121 us
    all_to_all x1, starting transfers between devices, shards(): sums = lax.all_to_all(part, TEAM, split_axis=0, concat_axis=0, tiled=True)  10.5 us
    pallas_call x1, Pallas kernels, shards(): pl.pallas_call(functools.partial(bucket_kernel, rows, slots), grid=(steps...  4.4 us
    pallas_call x1, Pallas kernels, shards(): pl.pallas_call(functools.partial(final_kernel, seq_devs, team_axes, ratio...  3.2 us
  transfers between devices with their start and end apart: 1, of which 1 were waited for; matrix products, arithmetic and copies ran while one was open for 0% of the time, Pallas kernels for 3%

profile of v10, /device:TPU:1, one launch (start us, length us, event | category | flops | bytes accessed | tf_op | source)
XLA Modules:
  0.0 145.5 jit_solution(1493093051067461137)
XLA Ops:
  0.0 2.5 %part.1 = f32[32,4,128]{2,1,0:T(4,128)} custom-call(s32[8]{0:T(128)} %lengths_ref.3, bf16[64,16384]{1,0:T(8,128)(2,1)} %x_ref.3), custom_call_target="tpu_custom_call" | custom-call | tf_op jit(solution)/shard_map/part/pallas_call | solution.py:164
  2.5 10.5 %all-to-all-start = ((f32[32,4,128]{2,1,0:T(4,128)}), f32[32,4,128]{2,1,0:T(4,128)S(1)}, u32[]{:S(2)}, u32[]{:S(2)}) async-start(f32[32,4,128]{2,1,0:T(4,128)} %part.1), calls=%async_computation | async-start | bytes 131072 | tf_op jit(solution)/shard_map/all_to_all | solution.py:174
  13.0 4.4 %bucket.1.tag_ref = bf16[64,8,2,2176]{3,2,1,0:T(2,128)(2,1)} custom-call(s32[8]{0:T(128)} %lengths_ref.3, s32[1,64]{1,0:T(1,128)} %bitcast.6, s32[1,64]{1,0:T(1,128)} %bitcast.7, bf16[64,16384]{1,0:T(8,128)(2,1)} %x_ref.3), custom_call_target="tpu_custom_call" | custom-call | flops 268435456 | bytes 8388608 | tf_op jit(solution)/shard_map/bucket/pallas_call | solution.py:177
  17.4 2.0 %all-to-all-done.sums_ref = f32[32,4,128]{2,1,0:T(4,128)S(1)} async-done(((f32[32,4,128]{2,1,0:T(4,128)}), f32[32,4,128]{2,1,0:T(4,128)S(1)}, u32[]{:S(2)}, u32[]{:S(2)}) %all-to-all-start) | async-done | bytes 65568 | tf_op jit(solution)/shard_map/all_to_all | solution.py:174
  19.5 1.8 %carry.1 = bf16[64,8,2,2176]{3,2,1,0:T(2,128)(2,1)} custom-call(f32[32,4,128]{2,1,0:T(4,128)S(1)} %all-to-all-done.sums_ref, bf16[64,8,2,2176]{3,2,1,0:T(2,128)(2,1)} %bucket.1.tag_ref), custom_call_target="tpu_custom_call", output_to_operand_aliasing={{}: (1, {})} | custom-call | tf_op jit(solution)/shard_map/carry/pallas_call | solution.py:192
  21.3 0.0 copy-start
  21.3 121.0 %all_to_all.10.got_ref = bf16[512,2,2176]{2,1,0:T(2,128)(2,1)S(1)} all-to-all(bf16[512,2,2176]{2,1,0:T(2,128)(2,1)} %bitcast.5), channel_id=1, replica_groups=mesh['z1'=2,'z0'=2,'core'=2,'yh'=4,'yl'=2,'x'=4,'zhi'=2] {'yh','yl','x',..., dimensions={0} | all-to-all | bytes 8912896 | tf_op jit(solution)/shard_map/all_to_all | solution.py:207
  142.3 0.0 copy-done
  142.3 3.2 %final.1 = f32[2048,256]{1,0:T(8,128)} custom-call(f32[16,128]{1,0:T(8,128)S(1)} %bitcast.4, bf16[512,2,2176]{2,1,0:T(2,128)(2,1)S(1)} %all_to_all.10.got_ref), custom_call_target="tpu_custom_call" | custom-call | tf_op jit(solution)/shard_map/final/pallas_call | solution.py:211
Async XLA Ops:
  2.5 16.9 %all-to-all-start = ((f32[32,4,128]{2,1,0:T(4,128)}), f32[32,4,128]{2,1,0:T(4,128)S(1)}, u32[]{:S(2)}, u32[]{:S(2)}) async-start(f32[32,4,128]{2,1,0:T(4,128)} %part.1), calls=%async_computation | async-start | bytes 131072 | tf_op jit(solution)/shard_map/all_to_all | solution.py:174
  21.3 121.1 %copy-start = (f32[2048]{0:T(1024)S(1)}, f32[2048]{0:T(1024)}, u32[]{:S(2)}) copy-start(f32[2048]{0:T(1024)} %param.9) | copy-start | bytes 24580
